TPU v7x, 32 devices: a whole 2x2x4 slice. The times are simulated.
32 devices in a mesh: groups: 2 (over x), gx: 8 (over z, y), yz: 2 (over core).
Axes of the slice: x: 2, y: 2, z: 4, core: 2. Of those that a mesh axis runs over, the one named last changes fastest.
Arguments:
- tokens: bfloat16 [768, 18432], P(('groups', 'yz'), 'gx'), parts along dimension 0, may hold values from -100 to 100
- query_weight: bfloat16 [18432, 6144], P('gx', 'yz'), may hold values from -0.046875 to 0.046875
- keyvalue_weight: bfloat16 [18432, 512], P('gx'), may hold values from -0.046875 to 0.046875
- output_weight: bfloat16 [6144, 18432], P('yz', 'gx'), may hold values from -0.078125 to 0.078125
Outputs:
- attended: bfloat16 [768, 18432], P(('groups', 'yz'), 'gx'), parts along dimension 0
There are 2 independent parts, one for each index of `groups`. A program takes and returns all parts, laid end to end along the dimension named above; an argument that names none is the same for every part. Nothing has to cross between parts.
All inputs are finite; a program needn't handle non-finite values.
Results may differ from a plain program's by a relative error of at most 0.012.
The roundings to bfloat16 on the way count: a program that leaves them out, or rounds other values in their place, can miss the bound.
Values may be sent and summed in bfloat16 or wider, within the bound.
No kernel may reach another device: no remote copies, remote signals or barrier semaphores. Data moves between devices by JAX's collectives and lax.ppermute only.
A program may use at most 128 MiB of HBM per device.

v0:
```python
import jax
import jax.numpy as jnp
from jax import lax
from jax.sharding import PartitionSpec as P

HEAD = 256
PROMPTS = 1


def on_device(tokens, query_weight, keyvalue_weight, output_weight):
    whole = lax.all_gather(tokens, "yz", axis=0, tiled=True)
    total = whole.shape[0]
    span = total // lax.axis_size("gx")
    first = lax.axis_index("gx") * span
    width = query_weight.shape[1]
    joined = lax.psum_scatter(
        jnp.concatenate(
            [
                jnp.dot(whole, query_weight, preferred_element_type=jnp.float32),
                jnp.dot(whole, keyvalue_weight, preferred_element_type=jnp.float32),
            ],
            axis=1,
        ),
        "gx",
        scatter_dimension=0,
        tiled=True,
    )
    query = joined[:, :width].astype(jnp.bfloat16)
    own_keys = joined[:, width:].astype(jnp.bfloat16)
    keyvalue = lax.all_gather(own_keys, "gx", axis=0, tiled=True)
    local_heads = width // HEAD
    grouped = query.reshape(span, local_heads, HEAD)
    keys = keyvalue[:, :HEAD]
    values = keyvalue[:, HEAD:]
    scores = jnp.einsum(
        "qhd,kd->qhk", grouped, keys, preferred_element_type=jnp.float32
    ) * HEAD ** (-0.5)
    query_pos = first + jnp.arange(span)
    key_pos = jnp.arange(total)
    allowed = (key_pos[None, :] <= query_pos[:, None]) & (
        key_pos[None, :] % PROMPTS == query_pos[:, None] % PROMPTS
    )
    scores = jnp.where(allowed[:, None, :], scores, -1e30)
    probs = jax.nn.softmax(scores, axis=-1).astype(jnp.bfloat16)
    mixed = jnp.einsum("qhk,kd->qhd", probs, values, preferred_element_type=jnp.float32)
    mixed = mixed.astype(jnp.bfloat16).reshape(span, width)
    partial_value = jnp.dot(
        lax.all_gather(mixed, "gx", axis=0, tiled=True),
        output_weight,
        preferred_element_type=jnp.float32,
    )
    return lax.psum_scatter(partial_value, "yz", scatter_dimension=0, tiled=True).astype(
        jnp.bfloat16
    )


def solution(mesh):
    return jax.shard_map(
        on_device,
        mesh=mesh,
        in_specs=(P(("groups", "yz"), "gx"), P("gx", "yz"), P("gx", None), P("yz", "gx")),
        out_specs=P(("groups", "yz"), "gx"),
        check_vma=False,
    )
```

profile of v0, /device:TPU:0, one launch (start us, length us, event | category | flops | bytes accessed | tf_op | source)
XLA Modules:
  0.0 264.0 jit_solution(410260252819142441)
XLA Ops:
  6.5 0.0 copy-start
  6.5 0.0 all-gather.3.cloned.1.call-start
  6.5 0.7 all-gather.3.cloned.1.call-update
  7.3 0.0 reduce-scatter.3.cloned.1.call-start
  7.3 14.4 %all-gather.3.cloned.1.call-done = bf16[384,2304]{1,0:T(8,128)(2,1)} async-done(((bf16[192,2304]{1,0:T(8,128)(2,1)}), bf16[384,2304]{1,0:T(8,128)(2,1)}) %all-gather.3.cloned.1.call-update) | async-done | bytes 1769488 | tf_op jit(solution)/shard_map/all_gather | solution.py:11
  21.7 0.0 copy-start.1
  21.7 11.2 %fusion.17 = f32[384,3072]{1,0:T(8,128)S(1)} fusion(bf16[384,2304]{1,0:T(8,128)(2,1)} %all-gather.3.cloned.1.call-done, bf16[2304,3072]{1,0:T(8,128)(2,1)} %param.5), kind=kOutput, calls=%fused_computation.19 | convolution fusion | flops 5435817984 | bytes 20643840 | tf_op jit(solution)/shard_map/dot_general | solution.py:19
  32.9 0.0 copy-done
  32.9 0.0 copy-done.1
  33.0 1.1 fusion.18
  34.0 2.9 %pad_maximum_fusion = f32[384,3584]{1,0:T(8,128)} fusion(f32[384,512]{1,0:T(8,128)S(1)} %fusion.18, f32[384,3072]{1,0:T(8,128)S(1)} %fusion.17), kind=kLoop, calls=%fused_computation.1 | loop fusion | flops 1376256 | bytes 11010048 | tf_op jit(solution)/shard_map/concatenate | solution.py:17
  36.9 0.0 reduce-scatter.3.cloned.1.call-update
  36.9 0.0 all-gather.5.cloned.1.call-start
  37.0 0.1 iota_compare_fusion
  37.1 107.4 %reduce-scatter.3.cloned.1.call-done = f32[48,3584]{1,0:T(8,128)} async-done(((f32[384,3584]{1,0:T(8,128)}), f32[48,3584]{1,0:T(8,128)}) %reduce-scatter.3.cloned.1.call-update) | async-done | bytes 688144 | tf_op jit(solution)/shard_map/reduce_scatter | solution.py:16
  144.5 1.1 convert.4
  145.7 31.1 %all_gather.10 = bf16[384,512]{1,0:T(8,128)(2,1)S(1)} all-gather(bf16[48,512]{1,0:T(8,128)(2,1)S(1)} %slice.19), channel_id=1, replica_groups=mesh['groups'=2,'gx'=8,'yz'=2] {'gx'}, dimensions={0}, use_global_device_ids=true | all-gather | bytes 442368 | tf_op jit(solution)/shard_map/all_gather | solution.py:30
  176.7 1.4 fusion.14
  178.1 1.5 fusion.4
  179.6 0.7 copy.9
  180.4 0.0 all-gather.5.cloned.1.call-update
  180.4 0.0 reduce-scatter.5.cloned.1.call-start
  180.4 52.0 %all-gather.5.cloned.1.call-done = bf16[384,3072]{1,0:T(8,128)(2,1)} async-done(((bf16[48,3072]{1,0:T(8,128)(2,1)}), bf16[384,3072]{1,0:T(8,128)(2,1)}) %all-gather.5.cloned.1.call-update) | async-done | bytes 2359312 | tf_op jit(solution)/shard_map/all_gather | solution.py:48
  232.4 12.4 %fusion.19 = f32[384,2304]{1,0:T(8,128)} fusion(bf16[384,3072]{1,0:T(8,128)(2,1)} %all-gather.5.cloned.1.call-done, bf16[3072,2304]{1,0:T(8,128)(2,1)} %param.7), kind=kOutput, calls=%fused_computation.21 | convolution fusion | flops 5435817984 | bytes 20054016 | tf_op jit(solution)/shard_map/dot_general | solution.py:47
  244.8 0.0 reduce-scatter.5.cloned.1.call-update
  244.9 10.1 %reduce-scatter.5.cloned.1.call-done = f32[192,2304]{1,0:T(8,128)} async-done(((f32[384,2304]{1,0:T(8,128)}), f32[192,2304]{1,0:T(8,128)}) %reduce-scatter.5.cloned.1.call-update) | async-done | bytes 1769488 | tf_op jit(solution)/shard_map/reduce_scatter | solution.py:52
  255.0 2.5 convert_element_type.13
  (3 shorter events, 0.0 us)
Async XLA Ops:
  6.5 26.4 %copy-start = (bf16[2304,512]{1,0:T(8,128)(2,1)S(1)}, bf16[2304,512]{1,0:T(8,128)(2,1)}, u32[]{:S(2)}) copy-start(bf16[2304,512]{1,0:T(8,128)(2,1)} %param.6) | copy-start | bytes 7077892
  6.5 15.2 %all-gather.3.cloned.1.call-start = ((), (), s32[]{:S(2)}) async-start(), calls=%async_computation.2 | async-start | bytes 2654208 | tf_op jit(solution)/shard_map/all_gather | solution.py:11
  7.3 137.2 %reduce-scatter.3.cloned.1.call-start = ((), (), s32[]{:S(2)}) async-start(), calls=%async_computation.3 | async-start | bytes 6193152 | tf_op jit(solution)/shard_map/reduce_scatter | solution.py:16
  21.7 11.2 %copy-start.1 = (bf16[384,2304]{1,0:T(8,128)(2,1)S(1)}, bf16[384,2304]{1,0:T(8,128)(2,1)}, u32[]{:S(2)}) copy-start(bf16[384,2304]{1,0:T(8,128)(2,1)} %all-gather.3.cloned.1.call-done) | copy-start | bytes 5308420
  36.9 195.5 %all-gather.5.cloned.1.call-start = ((), (), s32[]{:S(2)}) async-start(), calls=%async_computation.4 | async-start | bytes 2654208 | tf_op jit(solution)/shard_map/all_gather | solution.py:48
  180.4 74.6 %reduce-scatter.5.cloned.1.call-start = ((), (), s32[]{:S(2)}) async-start(), calls=%async_computation.5 | async-start | bytes 5308416 | tf_op jit(solution)/shard_map/reduce_scatter | solution.py:52
Sparse Core Ops, SparseCore 0:
  8.9 12.7 all-gather.2
  37.0 107.4 reduce-scatter.2
  180.5 51.8 all-gather.4
  245.0 9.9 reduce-scatter.4
where the time goes:
time: 264 us
  waiting for transfers between devices  185 us (70%)
  blocking collectives  31.1 us (12%)
  matrix products  27.6 us (10%)
  between operations  13.2 us (5%)
  other arithmetic  6.55 us (2%)
    reduce_scatter x1, waiting for transfers between devices, on_device(): lax.psum_scatter(jnp.concatenate([jnp.dot(whole, query_weight, preferred_...  107 us
    all_gather x1, waiting for transfers between devices, on_device(): lax.all_gather(mixed, 'gx', axis=0, tiled=True)  52 us
    all_gather x1, blocking collectives, on_device(): keyvalue = lax.all_gather(own_keys, 'gx', axis=0, tiled=True)  31.1 us
    all_gather x1, waiting for transfers between devices, on_device(): whole = lax.all_gather(tokens, 'yz', axis=0, tiled=True)  14.4 us
    dot_general x1, matrix products, on_device(): jnp.dot(lax.all_gather(mixed, 'gx', axis=0, tiled=True), output_weight, p...  12.4 us
    dot_general x1, matrix products, on_device(): jnp.dot(whole, query_weight, preferred_element_type=jnp.float32)  11.2 us
    reduce_scatter x1, waiting for transfers between devices, on_device(): lax.psum_scatter(partial_value, 'yz', scatter_dimension=0, tiled=True)  10.1 us
  transfers between devices with their start and end apart: 4, of which 4 were waited for; matrix products, arithmetic and copies ran while one was open for 0% of the time, Pallas kernels for 0%

commit v1 on v0

v1 whole, which is shorter than its diff:
```python
import jax
import jax.numpy as jnp
from jax import lax
from jax.sharding import PartitionSpec as P

HEAD = 256
PROMPTS = 1
PARTS = 3
F32 = jnp.float32
BF16 = jnp.bfloat16
F16 = jnp.float16
SCALE = 0.5
LOW = 2048.0


def cube(n):
    m = n.bit_length() - 1
    return [1 << j if j < 2 else 3 << (j - 1) for j in range(m)]


def coordinates(index, m):
    bits = [(index >> j) & 1 for j in range(m)]
    out = list(bits)
    for j in range(m - 1, 1, -1):
        out[j - 1] = bits[j - 1] ^ out[j]
    return out


def exchange(x, mask, axis="gx"):
    n = lax.axis_size(axis)
    return lax.ppermute(x, axis, [(i, i ^ mask) for i in range(n)])


def split(x):
    half = x * SCALE
    high = lax.reduce_precision(half, 5, 10)
    low = (half - high) * LOW
    return jnp.concatenate([high.astype(F16), low.astype(F16)], axis=-1)


def join(x):
    c = x.shape[-1] // 2
    return (x[..., :c].astype(F32) + x[..., c:].astype(F32) * (1.0 / LOW)) * (1.0 / SCALE)


def pick(x, at, axis):
    return lax.dynamic_index_in_dim(x, at, axis, keepdims=False)


def on_device(tokens, query_weight, keyvalue_weight, output_weight):
    n = lax.axis_size("gx")
    masks = cube(n)
    m = len(masks)
    core = lax.axis_index("yz")
    where = coordinates(lax.axis_index("gx"), m)
    own = tokens.shape[0]
    total = own * lax.axis_size("yz")
    span = total // n
    width = query_weight.shape[1]
    cols = width // PARTS
    other = exchange(tokens, 1, "yz")
    kv = jnp.dot(tokens, keyvalue_weight, preferred_element_type=F32)
    whole = jnp.where(
        core == 0, jnp.concatenate([tokens, other], 0), jnp.concatenate([other, tokens], 0)
    )
    cubed = whole.reshape([2] * m + [span, whole.shape[1]])
    orders = [[(p * m // PARTS + j) % m for j in range(m)] for p in range(PARTS)]

    kvs = [kv[p * (own // PARTS) : (p + 1) * (own // PARTS)] for p in range(PARTS)]
    kept, got = [], []
    for p in range(PARTS):
        d = orders[p][0]
        w = query_weight[:, p * cols : (p + 1) * cols]
        rows = pick(cubed, 1 - where[d], d).reshape(total // 2, -1)
        send = (jnp.dot(rows, w, preferred_element_type=F32) * SCALE).astype(F16)
        got.append(exchange(jnp.concatenate([send, split(kvs[p])], 0), masks[d]))
    for p in range(PARTS):
        d = orders[p][0]
        w = query_weight[:, p * cols : (p + 1) * cols]
        rows = pick(cubed, where[d], d).reshape(total // 2, -1)
        kept.append(jnp.dot(rows, w, preferred_element_type=F32))
    left = [sorted(set(range(m)) - {orders[p][0]}) for p in range(PARTS)]
    for s in range(1, m + 1):
        for p in range(PARTS):
            size = kept[p].shape[0]
            kept[p] = kept[p] + got[p][:size].astype(F32) * (1.0 / SCALE)
            kvs[p] = kvs[p] + join(got[p][size:])
        if s == m:
            break
        for p in range(PARTS):
            d = orders[p][s]
            axis = left[p].index(d)
            left[p].remove(d)
            x = kept[p].reshape([2] * (m - s) + [span, cols])
            send = (pick(x, 1 - where[d], axis).reshape(-1, cols) * SCALE).astype(F16)
            kept[p] = pick(x, where[d], axis).reshape(-1, cols)
            got[p] = exchange(jnp.concatenate([send, split(kvs[p])], 0), masks[d])

    block = sum(where[d] << (m - 1 - d) for d in range(m))
    own_kv = jnp.concatenate(kvs, 0).astype(BF16)
    other_kv = exchange(own_kv, 1, "yz")
    keyvalue = jnp.where(
        core == 0, jnp.concatenate([own_kv, other_kv], 0), jnp.concatenate([other_kv, own_kv], 0)
    )
    keys = keyvalue[:, :HEAD]
    values = keyvalue[:, HEAD:]
    heads = cols // HEAD
    query_pos = block * span + jnp.arange(span)
    key_pos = jnp.arange(total)
    allowed = (key_pos[None, :] <= query_pos[:, None]) & (
        key_pos[None, :] % PROMPTS == query_pos[:, None] % PROMPTS
    )
    mixed = []
    for p in range(PARTS):
        grouped = kept[p].astype(BF16).reshape(span, heads, HEAD)
        scores = jnp.einsum("qhd,kd->hqk", grouped, keys, preferred_element_type=F32) * HEAD ** (
            -0.5
        )
        scores = jnp.where(allowed[None], scores, -1e30)
        probs = lax.optimization_barrier(jax.nn.softmax(scores, axis=-1).astype(BF16))
        out = jnp.einsum("hqk,kd->qhd", probs, values, preferred_element_type=F32)
        mixed.append(out.astype(BF16).reshape(span, cols))

    have = [[] for _ in range(PARTS)]
    for s in range(m - 1, -1, -1):
        received = [exchange(mixed[p], masks[orders[p][s]]) for p in range(PARTS)]
        for p in range(PARTS):
            d = orders[p][s]
            have[p] = sorted(have[p] + [d])
            axis = have[p].index(d)
            shape = [2] * (len(have[p]) - 1) + [span, cols]
            a, b = mixed[p].reshape(shape), received[p].reshape(shape)
            low, high = jnp.where(where[d] == 0, a, b), jnp.where(where[d] == 0, b, a)
            mixed[p] = jnp.stack([low, high], axis).reshape(-1, cols)
    mixed = jnp.concatenate(mixed, 1)
    theirs = lax.dynamic_slice_in_dim(mixed, (1 - core) * own, own, 0)
    mine = lax.dynamic_slice_in_dim(mixed, core * own, own, 0)
    send = jnp.dot(theirs, output_weight, preferred_element_type=F32)
    back = exchange(send, 1, "yz")
    return (jnp.dot(mine, output_weight, preferred_element_type=F32) + back).astype(BF16)


def solution(mesh):
    return jax.shard_map(
        on_device,
        mesh=mesh,
        in_specs=(P(("groups", "yz"), "gx"), P("gx", "yz"), P("gx", None), P("yz", "gx")),
        out_specs=P(("groups", "yz"), "gx"),
        check_vma=False,
    )
```

time: 264 us -> 149 us (0.56)
  waiting for transfers between devices: 185 us -> 72.6 us
  starting transfers between devices: 0.12 us -> 37.3 us
  blocking collectives: 31.1 us -> 0 us
  between operations: 13.2 us -> 0.57 us
  matrix products: 27.6 us -> 30.3 us
    reduce_scatter x2 -> x0, waiting for transfers between devices: 118 us -> none  [the longest x1 107 us: on_device(): lax.psum_scatter(jnp.concatenate([jnp.dot(whole, query_weight, preferred_...]
    ppermute x0 -> x21, waiting for transfers between devices: none -> 72.6 us  [exchange(): return lax.ppermute(x, axis, [(i, i ^ mask) for i in range(n)])]
    all_gather x2 -> x0, waiting for transfers between devices: 66.4 us -> none  [the longest x1 52 us: on_device(): lax.all_gather(mixed, 'gx', axis=0, tiled=True)]
    ppermute x0 -> x21, starting transfers between devices: none -> 37.3 us  [exchange(): return lax.ppermute(x, axis, [(i, i ^ mask) for i in range(n)])]
    all_gather x1 -> x0, blocking collectives: 31.1 us -> none  [on_device(): keyvalue = lax.all_gather(own_keys, 'gx', axis=0, tiled=True)]
    dot_general x4 -> x12, matrix products: 26.2 us -> 29.1 us  [the longest x1 9.81 us: on_device(): jnp.dot(mine, output_weight, preferred_element_type=F32) + back]
  transfers between devices with their start and end apart: 4 -> 21, of which waited for: 4 -> 14; matrix products, arithmetic and copies ran while one was open for 0% -> 7% of each run, Pallas kernels for 0% -> 0%
where the time goes in v1:
time: 149 us
  waiting for transfers between devices  72.6 us (49%)
  starting transfers between devices  37.3 us (25%)
  matrix products  30.3 us (20%)
  other arithmetic  6.39 us (4%)
  local copies, waits for them, and re-layouts  1.64 us (1%)
    ppermute x21, waiting for transfers between devices, exchange(): return lax.ppermute(x, axis, [(i, i ^ mask) for i in range(n)])  72.6 us
    ppermute x21, starting transfers between devices, exchange(): return lax.ppermute(x, axis, [(i, i ^ mask) for i in range(n)])  37.3 us
    dot_general x1, matrix products, on_device(): jnp.dot(mine, output_weight, preferred_element_type=F32) + back  9.81 us
    dot_general x1, matrix products, on_device(): send = jnp.dot(theirs, output_weight, preferred_element_type=F32)  7.64 us
    dot_general x3, matrix products, on_device(): send = (jnp.dot(rows, w, preferred_element_type=F32) * SCALE).astype(F16)  5.81 us
    dot_general x3, matrix products, on_device(): kept.append(jnp.dot(rows, w, preferred_element_type=F32))  3.4 us
  transfers between devices with their start and end apart: 21, of which 14 were waited for; matrix products, arithmetic and copies ran while one was open for 7% of the time, Pallas kernels for 0%

profile of v1, /device:TPU:0, one launch (start us, length us, event | category | flops | bytes accessed | tf_op | source)
XLA Modules:
  0.0 148.7 jit_solution(9506583185167196607)
XLA Ops:
  0.0 0.5 collective-permute-start
  0.5 1.1 copy-done
  1.7 1.8 %fusion.105 = f32[192,512]{1,0:T(8,128)S(1)} fusion(bf16[192,2304]{1,0:T(8,128)(2,1)} %param.4, bf16[2304,512]{1,0:T(8,128)(2,1)S(1)} %copy-done), kind=kOutput, calls=%fused_computation.201 | convolution fusion | flops 452984832 | bytes 3637248 | tf_op jit(solution)/shard_map/dot_general | solution.py:62
  3.6 2.1 %maximum_select_fusion = bf16[384,2304]{1,0:T(8,128)(2,1)S(1)} fusion(bf16[192,2304]{1,0:T(8,128)(2,1)} %collective-permute-done, bf16[192,2304]{1,0:T(8,128)(2,1)S(1)} %copy-done.3, pred[]{:T(512)S(6)} %eq.18), kind=kLoop, calls=%fused_computation.18 | loop fusion | flops 7962624 | bytes 3538945 | tf_op jit(solution)/shard_map/jit(_where)/select_n | solution.py:63
  5.7 0.1 constant_dynamic-slice_fusion.7
  5.8 3.6 %fusion.31 = f16[192,1024]{1,0:T(8,128)(2,1)S(1)} fusion(bf16[192,2304]{1,0:T(8,128)(2,1)S(1)} %bitcast.187, bf16[2304,3072]{1,0:T(8,128)(2,1)} %param.5), kind=kOutput, calls=%fused_computation.24 | convolution fusion | flops 906362880 | bytes 5996544 | tf_op jit(solution)/shard_map/dot_general | solution.py:75
  9.5 0.1 maximum_maximum_fusion
  9.6 3.0 %collective-permute-start.1 = (f16[256,1024]{1,0:T(8,128)(2,1)S(1)}, f16[256,1024]{1,0:T(8,128)(2,1)S(1)}, u32[]{:S(2)}, u32[]{:S(2)}) collective-permute-start(f16[256,1024]{1,0:T(8,128)(2,1)S(1)} %maximum_maximum_fusion), channel_id=1, source_target_pairs={{0,2},{2,0},{4,6},{6,4},{8,10},{10,8},{12,14},{14,12},{1,3},{3,1},... | collective-permute-start | bytes 1572872 | tf_op jit(solution)/shard_map/ppermute | solution.py:31
  12.6 0.1 constant_dynamic-slice_fusion.4
  12.7 0.1 constant_dynamic-slice_fusion.1
  12.9 1.1 fusion.28
  14.0 10.6 %collective-permute-done.1 = f16[256,1024]{1,0:T(8,128)(2,1)S(1)} collective-permute-done((f16[256,1024]{1,0:T(8,128)(2,1)S(1)}, f16[256,1024]{1,0:T(8,128)(2,1)S(1)}, u32[]{:S(2)}, u32[]{:S(2)}) %collective-permute-start.1) | collective-permute-done | bytes 524320 | tf_op jit(solution)/shard_map/ppermute | solution.py:31
  24.6 1.1 multiply_add_fusion.2
  25.7 0.3 reduce-precision_convert_fusion.7
  26.2 1.9 %collective-permute-start.2 = (f16[160,1024]{1,0:T(8,128)(2,1)S(1)}, f16[160,1024]{1,0:T(8,128)(2,1)S(1)}, u32[]{:S(2)}, u32[]{:S(2)}) collective-permute-start(f16[160,1024]{1,0:T(8,128)(2,1)S(1)} %maximum_maximum_fusion.3), channel_id=1, source_target_pairs={{0,4},{2,6},{4,0},{6,2},{8,12},{10,14},{12,8},{14,10},{1,5},{3,7},... | collective-permute-start | bytes 983048 | tf_op jit(solution)/shard_map/ppermute | solution.py:31
  28.1 1.1 fusion.25
  29.2 0.1 maximum_maximum_fusion.1
  29.3 0.3 collective-permute-start.4
  29.6 0.1 maximum_maximum_fusion.2
  29.7 3.9 %collective-permute-start.7 = (f16[256,1024]{1,0:T(8,128)(2,1)S(1)}, f16[256,1024]{1,0:T(8,128)(2,1)S(1)}, u32[]{:S(2)}, u32[]{:S(2)}) collective-permute-start(f16[256,1024]{1,0:T(8,128)(2,1)S(1)} %maximum_maximum_fusion.2), channel_id=1, source_target_pairs={{0,12},{2,14},{4,8},{6,10},{8,4},{10,6},{12,0},{14,2},{1,13},{3,15... | collective-permute-start | bytes 1572872 | tf_op jit(solution)/shard_map/ppermute | solution.py:31
  33.6 3.3 %collective-permute-done.2 = f16[160,1024]{1,0:T(8,128)(2,1)S(1)} collective-permute-done((f16[160,1024]{1,0:T(8,128)(2,1)S(1)}, f16[160,1024]{1,0:T(8,128)(2,1)S(1)}, u32[]{:S(2)}, u32[]{:S(2)}) %collective-permute-start.2) | collective-permute-done | bytes 327712 | tf_op jit(solution)/shard_map/ppermute | solution.py:31
  37.0 0.1 reduce-precision_convert_fusion.6
  37.2 3.9 %collective-permute-start.3 = (f16[112,1024]{1,0:T(8,128)(2,1)S(1)}, f16[112,1024]{1,0:T(8,128)(2,1)S(1)}, u32[]{:S(2)}, u32[]{:S(2)}) collective-permute-start(f16[112,1024]{1,0:T(8,128)(2,1)S(1)} %maximum_maximum_fusion.6), channel_id=1, source_target_pairs={{0,12},{2,14},{4,8},{6,10},{8,4},{10,6},{12,0},{14,2},{1,13},{3,15... | collective-permute-start | bytes 688136 | tf_op jit(solution)/shard_map/ppermute | solution.py:31
  41.1 6.4 %collective-permute-done.4 = f16[256,1024]{1,0:T(8,128)(2,1)S(1)} collective-permute-done((f16[256,1024]{1,0:T(8,128)(2,1)S(1)}, f16[256,1024]{1,0:T(8,128)(2,1)S(1)}, u32[]{:S(2)}, u32[]{:S(2)}) %collective-permute-start.4) | collective-permute-done | bytes 524320 | tf_op jit(solution)/shard_map/ppermute | solution.py:31
  47.5 1.2 multiply_add_fusion.1
  48.7 13.0 %collective-permute-done.7 = f16[256,1024]{1,0:T(8,128)(2,1)S(1)} collective-permute-done((f16[256,1024]{1,0:T(8,128)(2,1)S(1)}, f16[256,1024]{1,0:T(8,128)(2,1)S(1)}, u32[]{:S(2)}, u32[]{:S(2)}) %collective-permute-start.7) | collective-permute-done | bytes 524320 | tf_op jit(solution)/shard_map/ppermute | solution.py:31
  61.7 0.2 reduce-precision_convert_fusion.4
  62.1 9.2 %collective-permute-start.5 = (f16[160,1024]{1,0:T(8,128)(2,1)S(1)}, f16[160,1024]{1,0:T(8,128)(2,1)S(1)}, u32[]{:S(2)}, u32[]{:S(2)}) collective-permute-start(f16[160,1024]{1,0:T(8,128)(2,1)S(1)} %maximum_maximum_fusion.4), channel_id=1, source_target_pairs={{0,12},{2,14},{4,8},{6,10},{8,4},{10,6},{12,0},{14,2},{1,13},{3,15... | collective-permute-start | bytes 983048 | tf_op jit(solution)/shard_map/ppermute | solution.py:31
  71.4 1.2 multiply_add_fusion
  72.7 1.5 %collective-permute-start.8 = (f16[160,1024]{1,0:T(8,128)(2,1)S(1)}, f16[160,1024]{1,0:T(8,128)(2,1)S(1)}, u32[]{:S(2)}, u32[]{:S(2)}) collective-permute-start(f16[160,1024]{1,0:T(8,128)(2,1)S(1)} %maximum_maximum_fusion.5), channel_id=1, source_target_pairs={{0,2},{2,0},{4,6},{6,4},{8,10},{10,8},{12,14},{14,12},{1,3},{3,1},... | collective-permute-start | bytes 983048 | tf_op jit(solution)/shard_map/ppermute | solution.py:31
  74.3 2.1 %collective-permute-done.5 = f16[160,1024]{1,0:T(8,128)(2,1)S(1)} collective-permute-done((f16[160,1024]{1,0:T(8,128)(2,1)S(1)}, f16[160,1024]{1,0:T(8,128)(2,1)S(1)}, u32[]{:S(2)}, u32[]{:S(2)}) %collective-permute-start.5) | collective-permute-done | bytes 327712 | tf_op jit(solution)/shard_map/ppermute | solution.py:31
  76.5 0.1 reduce-precision_convert_fusion.3
  76.7 1.6 %collective-permute-start.6 = (f16[112,1024]{1,0:T(8,128)(2,1)S(1)}, f16[112,1024]{1,0:T(8,128)(2,1)S(1)}, u32[]{:S(2)}, u32[]{:S(2)}) collective-permute-start(f16[112,1024]{1,0:T(8,128)(2,1)S(1)} %maximum_maximum_fusion.7), channel_id=1, source_target_pairs={{0,2},{2,0},{4,6},{6,4},{8,10},{10,8},{12,14},{14,12},{1,3},{3,1},... | collective-permute-start | bytes 688136 | tf_op jit(solution)/shard_map/ppermute | solution.py:31
  78.3 1.5 %collective-permute-done.8 = f16[160,1024]{1,0:T(8,128)(2,1)S(1)} collective-permute-done((f16[160,1024]{1,0:T(8,128)(2,1)S(1)}, f16[160,1024]{1,0:T(8,128)(2,1)S(1)}, u32[]{:S(2)}, u32[]{:S(2)}) %collective-permute-start.8) | collective-permute-done | bytes 327712 | tf_op jit(solution)/shard_map/ppermute | solution.py:31
  79.8 0.1 reduce-precision_convert_fusion
  80.1 1.1 collective-permute-start.9
  81.2 1.6 %collective-permute-done.6 = f16[112,1024]{1,0:T(8,128)(2,1)S(1)} collective-permute-done((f16[112,1024]{1,0:T(8,128)(2,1)S(1)}, f16[112,1024]{1,0:T(8,128)(2,1)S(1)}, u32[]{:S(2)}, u32[]{:S(2)}) %collective-permute-start.6) | collective-permute-done | bytes 229408 | tf_op jit(solution)/shard_map/ppermute | solution.py:31
  82.9 3.7 %collective-permute-done.9 = f16[112,1024]{1,0:T(8,128)(2,1)S(1)} collective-permute-done((f16[112,1024]{1,0:T(8,128)(2,1)S(1)}, f16[112,1024]{1,0:T(8,128)(2,1)S(1)}, u32[]{:S(2)}, u32[]{:S(2)}) %collective-permute-start.9) | collective-permute-done | bytes 229408 | tf_op jit(solution)/shard_map/ppermute | solution.py:31
  86.8 1.4 collective-permute-done.10
  88.2 0.1 maximum_select_fusion.1
  88.3 0.4 fusion.98
  88.8 0.2 fusion.49
  89.1 2.0 %collective-permute-start.11 = (bf16[48,1024]{1,0:T(8,128)(2,1)S(1)}, bf16[48,1024]{1,0:T(8,128)(2,1)S(1)}, u32[]{:S(2)}, u32[]{:S(2)}) collective-permute-start(bf16[48,1024]{1,0:T(8,128)(2,1)S(1)} %bitcast.202), channel_id=1, source_target_pairs={{0,12},{2,14},{4,8},{6,10},{8,4},{10,6},{12,0},{14,2},{1,13},{3,15... | collective-permute-start | bytes 294920 | tf_op jit(solution)/shard_map/ppermute | solution.py:31
  91.1 0.4 fusion.97
  91.5 0.1 divide_convert_fusion.1
  91.6 0.2 fusion.50
  91.8 0.6 collective-permute-start.14
  92.4 0.4 fusion.96
  92.9 0.2 fusion.51
  93.2 0.3 collective-permute-start.17
  93.5 2.4 %collective-permute-done.11 = bf16[48,1024]{1,0:T(8,128)(2,1)S(1)} collective-permute-done((bf16[48,1024]{1,0:T(8,128)(2,1)S(1)}, bf16[48,1024]{1,0:T(8,128)(2,1)S(1)}, u32[]{:S(2)}, u32[]{:S(2)}) %collective-permute-start.11) | collective-permute-done | bytes 98336 | tf_op jit(solution)/shard_map/ppermute | solution.py:31
  96.0 2.1 %collective-permute-start.12 = (bf16[96,1024]{1,0:T(8,128)(2,1)S(1)}, bf16[96,1024]{1,0:T(8,128)(2,1)S(1)}, u32[]{:S(2)}, u32[]{:S(2)}) collective-permute-start(bf16[96,1024]{1,0:T(8,128)(2,1)S(1)} %bitcast.206), channel_id=1, source_target_pairs={{0,4},{2,6},{4,0},{6,2},{8,12},{10,14},{12,8},{14,10},{1,5},{3,7},... | collective-permute-start | bytes 589832 | tf_op jit(solution)/shard_map/ppermute | solution.py:31
  98.2 1.4 collective-permute-start.15
  99.7 0.6 collective-permute-start.18
  100.3 7.4 %collective-permute-done.15 = bf16[96,1024]{1,0:T(8,128)(2,1)S(1)} collective-permute-done((bf16[96,1024]{1,0:T(8,128)(2,1)S(1)}, bf16[96,1024]{1,0:T(8,128)(2,1)S(1)}, u32[]{:S(2)}, u32[]{:S(2)}) %collective-permute-start.15) | collective-permute-done | bytes 196640 | tf_op jit(solution)/shard_map/ppermute | solution.py:31
  107.8 1.1 collective-permute-start.16
  109.0 1.7 %collective-permute-start.19 = (bf16[192,1024]{1,0:T(8,128)(2,1)S(1)}, bf16[192,1024]{1,0:T(8,128)(2,1)S(1)}, u32[]{:S(2)}, u32[]{:S(2)}) collective-permute-start(bf16[192,1024]{1,0:T(8,128)(2,1)S(1)} %bitcast.195), channel_id=1, source_target_pairs={{0,12},{2,14},{4,8},{6,10},{8,4},{10,6},{12,0},{14,2},{1,13},{3,15... | collective-permute-start | bytes 1179656 | tf_op jit(solution)/shard_map/ppermute | solution.py:31
  110.8 0.5 collective-permute-start.13
  111.2 7.2 %collective-permute-done.16 = bf16[192,1024]{1,0:T(8,128)(2,1)S(1)} collective-permute-done((bf16[192,1024]{1,0:T(8,128)(2,1)S(1)}, bf16[192,1024]{1,0:T(8,128)(2,1)S(1)}, u32[]{:S(2)}, u32[]{:S(2)}) %collective-permute-start.16) | collective-permute-done | bytes 393248 | tf_op jit(solution)/shard_map/ppermute | solution.py:31
  118.7 8.2 %collective-permute-done.19 = bf16[192,1024]{1,0:T(8,128)(2,1)S(1)} collective-permute-done((bf16[192,1024]{1,0:T(8,128)(2,1)S(1)}, bf16[192,1024]{1,0:T(8,128)(2,1)S(1)}, u32[]{:S(2)}, u32[]{:S(2)}) %collective-permute-start.19) | collective-permute-done | bytes 393248 | tf_op jit(solution)/shard_map/ppermute | solution.py:31
  127.2 0.2 pad_maximum_fusion
  127.4 7.6 %fusion.37 = f32[192,2304]{1,0:T(8,128)S(1)} fusion(bf16[3072,2304]{1,0:T(8,128)(2,1)} %param.7, bf16[384,3072]{1,0:T(8,128)(2,1)S(1)} %pad_maximum_fusion, s32[]{:T(128)S(6)} %select_n.362), kind=kOutput, calls=%fused_computation.28 | convolution fusion | flops 2717908992 | bytes 17104900 | tf_op jit(solution)/shard_map/dot_general | solution.py:138
  135.1 3.8 %collective-permute-done.20 = f32[192,2304]{1,0:T(8,128)} collective-permute-done((f32[192,2304]{1,0:T(8,128)S(1)}, f32[192,2304]{1,0:T(8,128)}, u32[]{:S(2)}, u32[]{:S(2)}) %collective-permute-start.20) | collective-permute-done | bytes 1769504 | tf_op jit(solution)/shard_map/ppermute | solution.py:31
  138.9 9.8 %fusion.15 = bf16[192,2304]{1,0:T(8,128)(2,1)} fusion(f32[192,2304]{1,0:T(8,128)} %collective-permute-done.20, bf16[3072,2304]{1,0:T(8,128)(2,1)} %param.7, bf16[384,3072]{1,0:T(8,128)(2,1)} %copy-done.2, s32[]{:T(128)S(6)} %select_n.361), kind=kOutput, calls=%fused_computation.16 | convolution fusion | flops 2718793728 | bytes 17989636 | tf_op jit(solution)/shard_map/dot_general | solution.py:140
  (71 shorter events, 3.0 us)
Async XLA Ops:
  0.0 1.7 %copy-start = (bf16[2304,512]{1,0:T(8,128)(2,1)S(1)}, bf16[2304,512]{1,0:T(8,128)(2,1)}, u32[]{:S(2)}) copy-start(bf16[2304,512]{1,0:T(8,128)(2,1)} %param.6) | copy-start | bytes 7077892
  0.0 3.6 %copy-start.3 = (bf16[192,2304]{1,0:T(8,128)(2,1)S(1)}, bf16[192,2304]{1,0:T(8,128)(2,1)}, u32[]{:S(2)}) copy-start(bf16[192,2304]{1,0:T(8,128)(2,1)} %param.4) | copy-start | bytes 2654212
  0.0 3.6 %collective-permute-start = (bf16[192,2304]{1,0:T(8,128)(2,1)}, bf16[192,2304]{1,0:T(8,128)(2,1)}, u32[]{:S(2)}, u32[]{:S(2)}) collective-permute-start(bf16[192,2304]{1,0:T(8,128)(2,1)} %param.4), channel_id=1, source_target_pairs={{0,1},{1,0},{2,3},{3,2},{4,5},{5,4},{6,7},{7,6},{8,9},{9,8},{10,11... | collective-permute-start | bytes 2654216 | tf_op jit(solution)/shard_map/ppermute | solution.py:31
  5.8 7.1 %copy-start.4 = (bf16[2304,3072]{1,0:T(8,128)(2,1)S(1)}, bf16[2304,3072]{1,0:T(8,128)(2,1)}, u32[]{:S(2)}) copy-start(bf16[2304,3072]{1,0:T(8,128)(2,1)} %param.5) | copy-start | bytes 42467332
  9.6 15.0 %collective-permute-start.1 = (f16[256,1024]{1,0:T(8,128)(2,1)S(1)}, f16[256,1024]{1,0:T(8,128)(2,1)S(1)}, u32[]{:S(2)}, u32[]{:S(2)}) collective-permute-start(f16[256,1024]{1,0:T(8,128)(2,1)S(1)} %maximum_maximum_fusion), channel_id=1, source_target_pairs={{0,2},{2,0},{4,6},{6,4},{8,10},{10,8},{12,14},{14,12},{1,3},{3,1},... | collective-permute-start | bytes 1572872 | tf_op jit(solution)/shard_map/ppermute | solution.py:31
  26.2 10.7 %collective-permute-start.2 = (f16[160,1024]{1,0:T(8,128)(2,1)S(1)}, f16[160,1024]{1,0:T(8,128)(2,1)S(1)}, u32[]{:S(2)}, u32[]{:S(2)}) collective-permute-start(f16[160,1024]{1,0:T(8,128)(2,1)S(1)} %maximum_maximum_fusion.3), channel_id=1, source_target_pairs={{0,4},{2,6},{4,0},{6,2},{8,12},{10,14},{12,8},{14,10},{1,5},{3,7},... | collective-permute-start | bytes 983048 | tf_op jit(solution)/shard_map/ppermute | solution.py:31
  29.3 18.2 %collective-permute-start.4 = (f16[256,1024]{1,0:T(8,128)(2,1)S(1)}, f16[256,1024]{1,0:T(8,128)(2,1)S(1)}, u32[]{:S(2)}, u32[]{:S(2)}) collective-permute-start(f16[256,1024]{1,0:T(8,128)(2,1)S(1)} %maximum_maximum_fusion.1), channel_id=1, source_target_pairs={{0,4},{2,6},{4,0},{6,2},{8,12},{10,14},{12,8},{14,10},{1,5},{3,7},... | collective-permute-start | bytes 1572872 | tf_op jit(solution)/shard_map/ppermute | solution.py:31
  29.7 32.0 %collective-permute-start.7 = (f16[256,1024]{1,0:T(8,128)(2,1)S(1)}, f16[256,1024]{1,0:T(8,128)(2,1)S(1)}, u32[]{:S(2)}, u32[]{:S(2)}) collective-permute-start(f16[256,1024]{1,0:T(8,128)(2,1)S(1)} %maximum_maximum_fusion.2), channel_id=1, source_target_pairs={{0,12},{2,14},{4,8},{6,10},{8,4},{10,6},{12,0},{14,2},{1,13},{3,15... | collective-permute-start | bytes 1572872 | tf_op jit(solution)/shard_map/ppermute | solution.py:31
  37.2 37.0 %collective-permute-start.3 = (f16[112,1024]{1,0:T(8,128)(2,1)S(1)}, f16[112,1024]{1,0:T(8,128)(2,1)S(1)}, u32[]{:S(2)}, u32[]{:S(2)}) collective-permute-start(f16[112,1024]{1,0:T(8,128)(2,1)S(1)} %maximum_maximum_fusion.6), channel_id=1, source_target_pairs={{0,12},{2,14},{4,8},{6,10},{8,4},{10,6},{12,0},{14,2},{1,13},{3,15... | collective-permute-start | bytes 688136 | tf_op jit(solution)/shard_map/ppermute | solution.py:31
  62.1 14.3 %collective-permute-start.5 = (f16[160,1024]{1,0:T(8,128)(2,1)S(1)}, f16[160,1024]{1,0:T(8,128)(2,1)S(1)}, u32[]{:S(2)}, u32[]{:S(2)}) collective-permute-start(f16[160,1024]{1,0:T(8,128)(2,1)S(1)} %maximum_maximum_fusion.4), channel_id=1, source_target_pairs={{0,12},{2,14},{4,8},{6,10},{8,4},{10,6},{12,0},{14,2},{1,13},{3,15... | collective-permute-start | bytes 983048 | tf_op jit(solution)/shard_map/ppermute | solution.py:31
  72.7 7.1 %collective-permute-start.8 = (f16[160,1024]{1,0:T(8,128)(2,1)S(1)}, f16[160,1024]{1,0:T(8,128)(2,1)S(1)}, u32[]{:S(2)}, u32[]{:S(2)}) collective-permute-start(f16[160,1024]{1,0:T(8,128)(2,1)S(1)} %maximum_maximum_fusion.5), channel_id=1, source_target_pairs={{0,2},{2,0},{4,6},{6,4},{8,10},{10,8},{12,14},{14,12},{1,3},{3,1},... | collective-permute-start | bytes 983048 | tf_op jit(solution)/shard_map/ppermute | solution.py:31
  76.7 6.1 %collective-permute-start.6 = (f16[112,1024]{1,0:T(8,128)(2,1)S(1)}, f16[112,1024]{1,0:T(8,128)(2,1)S(1)}, u32[]{:S(2)}, u32[]{:S(2)}) collective-permute-start(f16[112,1024]{1,0:T(8,128)(2,1)S(1)} %maximum_maximum_fusion.7), channel_id=1, source_target_pairs={{0,2},{2,0},{4,6},{6,4},{8,10},{10,8},{12,14},{14,12},{1,3},{3,1},... | collective-permute-start | bytes 688136 | tf_op jit(solution)/shard_map/ppermute | solution.py:31
  80.1 6.4 %collective-permute-start.9 = (f16[112,1024]{1,0:T(8,128)(2,1)S(1)}, f16[112,1024]{1,0:T(8,128)(2,1)S(1)}, u32[]{:S(2)}, u32[]{:S(2)}) collective-permute-start(f16[112,1024]{1,0:T(8,128)(2,1)S(1)} %maximum_maximum_fusion.8), channel_id=1, source_target_pairs={{0,4},{2,6},{4,0},{6,2},{8,12},{10,14},{12,8},{14,10},{1,5},{3,7},... | collective-permute-start | bytes 688136 | tf_op jit(solution)/shard_map/ppermute | solution.py:31
  86.7 1.5 %collective-permute-start.10 = (bf16[192,512]{1,0:T(8,128)(2,1)S(1)}, bf16[192,512]{1,0:T(8,128)(2,1)S(1)}, u32[]{:S(2)}, u32[]{:S(2)}) collective-permute-start(bf16[192,512]{1,0:T(8,128)(2,1)S(1)} %pad_maximum_fusion.10), channel_id=1, source_target_pairs={{0,1},{1,0},{2,3},{3,2},{4,5},{5,4},{6,7},{7,6},{8,9},{9,8},{10,11... | collective-permute-start | bytes 589832 | tf_op jit(solution)/shard_map/ppermute | solution.py:31
  89.1 6.8 %collective-permute-start.11 = (bf16[48,1024]{1,0:T(8,128)(2,1)S(1)}, bf16[48,1024]{1,0:T(8,128)(2,1)S(1)}, u32[]{:S(2)}, u32[]{:S(2)}) collective-permute-start(bf16[48,1024]{1,0:T(8,128)(2,1)S(1)} %bitcast.202), channel_id=1, source_target_pairs={{0,12},{2,14},{4,8},{6,10},{8,4},{10,6},{12,0},{14,2},{1,13},{3,15... | collective-permute-start | bytes 294920 | tf_op jit(solution)/shard_map/ppermute | solution.py:31
  91.8 6.3 %collective-permute-start.14 = (bf16[48,1024]{1,0:T(8,128)(2,1)S(1)}, bf16[48,1024]{1,0:T(8,128)(2,1)S(1)}, u32[]{:S(2)}, u32[]{:S(2)}) collective-permute-start(bf16[48,1024]{1,0:T(8,128)(2,1)S(1)} %bitcast.200), channel_id=1, source_target_pairs={{0,2},{2,0},{4,6},{6,4},{8,10},{10,8},{12,14},{14,12},{1,3},{3,1},... | collective-permute-start | bytes 294920 | tf_op jit(solution)/shard_map/ppermute | solution.py:31
  93.2 6.5 %collective-permute-start.17 = (bf16[48,1024]{1,0:T(8,128)(2,1)S(1)}, bf16[48,1024]{1,0:T(8,128)(2,1)S(1)}, u32[]{:S(2)}, u32[]{:S(2)}) collective-permute-start(bf16[48,1024]{1,0:T(8,128)(2,1)S(1)} %bitcast.204), channel_id=1, source_target_pairs={{0,4},{2,6},{4,0},{6,2},{8,12},{10,14},{12,8},{14,10},{1,5},{3,7},... | collective-permute-start | bytes 294920 | tf_op jit(solution)/shard_map/ppermute | solution.py:31
  96.0 14.7 %collective-permute-start.12 = (bf16[96,1024]{1,0:T(8,128)(2,1)S(1)}, bf16[96,1024]{1,0:T(8,128)(2,1)S(1)}, u32[]{:S(2)}, u32[]{:S(2)}) collective-permute-start(bf16[96,1024]{1,0:T(8,128)(2,1)S(1)} %bitcast.206), channel_id=1, source_target_pairs={{0,4},{2,6},{4,0},{6,2},{8,12},{10,14},{12,8},{14,10},{1,5},{3,7},... | collective-permute-start | bytes 589832 | tf_op jit(solution)/shard_map/ppermute | solution.py:31
  98.2 9.5 %collective-permute-start.15 = (bf16[96,1024]{1,0:T(8,128)(2,1)S(1)}, bf16[96,1024]{1,0:T(8,128)(2,1)S(1)}, u32[]{:S(2)}, u32[]{:S(2)}) collective-permute-start(bf16[96,1024]{1,0:T(8,128)(2,1)S(1)} %bitcast.207), channel_id=1, source_target_pairs={{0,12},{2,14},{4,8},{6,10},{8,4},{10,6},{12,0},{14,2},{1,13},{3,15... | collective-permute-start | bytes 589832 | tf_op jit(solution)/shard_map/ppermute | solution.py:31
  99.7 9.2 %collective-permute-start.18 = (bf16[96,1024]{1,0:T(8,128)(2,1)S(1)}, bf16[96,1024]{1,0:T(8,128)(2,1)S(1)}, u32[]{:S(2)}, u32[]{:S(2)}) collective-permute-start(bf16[96,1024]{1,0:T(8,128)(2,1)S(1)} %bitcast.208), channel_id=1, source_target_pairs={{0,2},{2,0},{4,6},{6,4},{8,10},{10,8},{12,14},{14,12},{1,3},{3,1},... | collective-permute-start | bytes 589832 | tf_op jit(solution)/shard_map/ppermute | solution.py:31
  107.8 10.7 %collective-permute-start.16 = (bf16[192,1024]{1,0:T(8,128)(2,1)S(1)}, bf16[192,1024]{1,0:T(8,128)(2,1)S(1)}, u32[]{:S(2)}, u32[]{:S(2)}) collective-permute-start(bf16[192,1024]{1,0:T(8,128)(2,1)S(1)} %bitcast.194), channel_id=1, source_target_pairs={{0,4},{2,6},{4,0},{6,2},{8,12},{10,14},{12,8},{14,10},{1,5},{3,7},... | collective-permute-start | bytes 1179656 | tf_op jit(solution)/shard_map/ppermute | solution.py:31
  109.0 17.9 %collective-permute-start.19 = (bf16[192,1024]{1,0:T(8,128)(2,1)S(1)}, bf16[192,1024]{1,0:T(8,128)(2,1)S(1)}, u32[]{:S(2)}, u32[]{:S(2)}) collective-permute-start(bf16[192,1024]{1,0:T(8,128)(2,1)S(1)} %bitcast.195), channel_id=1, source_target_pairs={{0,12},{2,14},{4,8},{6,10},{8,4},{10,6},{12,0},{14,2},{1,13},{3,15... | collective-permute-start | bytes 1179656 | tf_op jit(solution)/shard_map/ppermute | solution.py:31
  110.8 16.3 %collective-permute-start.13 = (bf16[192,1024]{1,0:T(8,128)(2,1)S(1)}, bf16[192,1024]{1,0:T(8,128)(2,1)S(1)}, u32[]{:S(2)}, u32[]{:S(2)}) collective-permute-start(bf16[192,1024]{1,0:T(8,128)(2,1)S(1)} %bitcast.196), channel_id=1, source_target_pairs={{0,2},{2,0},{4,6},{6,4},{8,10},{10,8},{12,14},{14,12},{1,3},{3,1},... | collective-permute-start | bytes 1179656 | tf_op jit(solution)/shard_map/ppermute | solution.py:31
  127.4 7.7 %copy-start.2 = (bf16[384,3072]{1,0:T(8,128)(2,1)}, bf16[384,3072]{1,0:T(8,128)(2,1)S(1)}, u32[]{:S(2)}) copy-start(bf16[384,3072]{1,0:T(8,128)(2,1)S(1)} %pad_maximum_fusion) | copy-start | bytes 7077892
  135.0 3.9 %collective-permute-start.20 = (f32[192,2304]{1,0:T(8,128)S(1)}, f32[192,2304]{1,0:T(8,128)}, u32[]{:S(2)}, u32[]{:S(2)}) collective-permute-start(f32[192,2304]{1,0:T(8,128)S(1)} %fusion.37), channel_id=1, source_target_pairs={{0,1},{1,0},{2,3},{3,2},{4,5},{5,4},{6,7},{7,6},{8,9},{9,8},{10,11... | collective-permute-start | bytes 5308424 | tf_op jit(solution)/shard_map/ppermute | solution.py:31
  138.9 9.8 %copy-start.1 = (bf16[2304,512]{1,0:T(8,128)(2,1)S(1)}, bf16[2304,512]{1,0:T(8,128)(2,1)}, u32[]{:S(2)}) copy-start(bf16[2304,512]{1,0:T(8,128)(2,1)} %param.6) | copy-start | bytes 7077892

commit v2 on v0

v2 whole, which is shorter than its diff:
```python
import jax
import jax.numpy as jnp
from jax import lax
from jax.sharding import PartitionSpec as P

HEAD = 256
PROMPTS = 1
GROUPS = 2
CHUNKS = 2
F32 = jnp.float32
BF16 = jnp.bfloat16
F16 = jnp.float16
SCALE = 0.5


def exchange(x, bit, axis="gx"):
    n = lax.axis_size(axis)
    return lax.ppermute(x, axis, [(i, i ^ (1 << bit)) for i in range(n)])


def pick(x, at, axis):
    return lax.dynamic_index_in_dim(x, at, axis, keepdims=False)


def half(x):
    return (x * SCALE).astype(F16)


def full(x):
    return x.astype(F32) * (1.0 / SCALE)


def on_device(tokens, query_weight, keyvalue_weight, output_weight):
    n = lax.axis_size("gx")
    m = n.bit_length() - 1
    core = lax.axis_index("yz")
    place = lax.axis_index("gx")
    where = [(place >> j) & 1 for j in range(m)]
    own = tokens.shape[0]
    total = 2 * own
    small = own // n
    span = 2 * small
    width = query_weight.shape[1]
    cols = width // (2 * GROUPS)
    orders = ((0, 1), (1, 0))

    def both(a, b, d, axis):
        first = where[d] == 0
        return jnp.stack([jnp.where(first, a, b), jnp.where(first, b, a)], axis)

    cube = [2] * m + [small]
    other = exchange(tokens, 0, "yz")
    kv = jnp.dot(tokens, keyvalue_weight, preferred_element_type=F32).reshape(cube + [-1])

    def kv_chain(x):
        for d in range(m - 1):
            got = exchange(pick(x, 1 - where[d], 0), d)
            x, got = yield pick(x, where[d], 0), got
            x = x + got
        x, got = yield x, exchange(x, m - 1)
        x = (x + got).astype(BF16)
        for d in range(m - 2, -1, -1):
            x, got = yield x, exchange(x, d)
            x = both(x, got, d, 0)
        x = x.reshape(own, 2 * HEAD)
        x, got = yield x, exchange(x, 0, "yz")
        return jnp.concatenate([x, got], 0)

    whole = jnp.stack([tokens, other]).reshape([2] + cube + [tokens.shape[1]])

    def product(g, part, mine):
        d = orders[part][0]
        first = (2 * g + part) * cols
        rows = pick(whole, where[d] if mine else 1 - where[d], 1 + d)
        return jnp.dot(
            rows.reshape(total // 2, -1),
            query_weight[:, first : first + cols],
            preferred_element_type=F32,
        )

    def query_chain(g):
        got = [exchange(half(product(g, part, False)), orders[part][0]) for part in range(2)]
        kept = [product(g, part, True) for part in range(2)]
        kept, got = yield kept, got
        after = []
        for part in range(2):
            x = (kept[part] + full(got[part])).reshape([2] * m + [small, cols])
            d = orders[part][1]
            got[part] = exchange(half(pick(x, 1 - where[d], 1)), d)
            after.append(pick(x, where[d], 1))
        kept, got = yield after, got
        x = jnp.concatenate([k + full(r) for k, r in zip(kept, got)], -1)
        for d in range(2, m):
            got = exchange(half(pick(x, 1 - where[d], 1)), d)
            x, got = yield pick(x, where[d], 1), got
            x = x + full(got)
        return x.astype(BF16)

    def attention(query, keyvalue):
        positions = jnp.arange(own)
        key_pos = jnp.concatenate([positions + core * own, positions + (1 - core) * own])
        block = sum(where[d] << (m - 1 - d) for d in range(m))
        query_pos = block * small + jnp.arange(small)
        query_pos = jnp.concatenate([query_pos + core * own, query_pos + (1 - core) * own])
        allowed = (key_pos[None, :] <= query_pos[:, None]) & (
            key_pos[None, :] % PROMPTS == query_pos[:, None] % PROMPTS
        )
        grouped = query.reshape(span, -1, HEAD)
        scores = jnp.einsum("qhd,kd->hqk", grouped, keyvalue[:, :HEAD], preferred_element_type=F32)
        scores = jnp.where(allowed[None], scores * HEAD ** (-0.5), -1e30)
        probs = lax.optimization_barrier(jax.nn.softmax(scores, axis=-1).astype(BF16))
        out = jnp.einsum("hqk,kd->qhd", probs, keyvalue[:, HEAD:], preferred_element_type=F32)
        return out.astype(BF16).reshape(2, small, 2 * cols)

    def mixed_chain(x):
        for d in range(m - 1, 1, -1):
            x, got = yield x, exchange(x, d)
            x = both(x, got, d, 1)
        parts = [x[..., :cols], x[..., cols:]]
        got = [exchange(parts[part], orders[part][1]) for part in range(2)]
        parts, got = yield parts, got
        parts = [both(parts[part], got[part], orders[part][1], 1) for part in range(2)]
        got = [exchange(parts[part], orders[part][0]) for part in range(2)]
        parts, got = yield parts, got
        parts = [both(parts[part], got[part], orders[part][0], 1 + orders[part][0]) for part in range(2)]
        return jnp.concatenate([x.reshape(total, cols) for x in parts], 1)

    class Chain:
        def __init__(self, chain):
            self.chain, self.done = chain, None
            self.state = next(chain)

        def go(self, *others):
            made = [o.state[0] for o in others]
            state, made = lax.optimization_barrier((self.state, made))
            for o, x in zip(others, made):
                o.state = (x, o.state[1])
            try:
                self.state = self.chain.send(state)
            except StopIteration as stop:
                self.done = stop.value

    k = Chain(kv_chain(kv))
    a, b = (Chain(query_chain(g)) for g in range(GROUPS))
    steps = m
    k.go(a, b)
    a.go(k, b)
    for s in range(1, steps):
        k.go(a, b)
        b.go(k, a)
        k.go(a, b)
        a.go(k, b)
    while k.done is None:
        k.go(b)
    a_mixed = Chain(mixed_chain(attention(a.done, k.done)))
    b.go(a_mixed)
    b_mixed = Chain(mixed_chain(attention(b.done, k.done)))
    for s in range(steps):
        a_mixed.go(b_mixed)
        if s < steps - 1:
            b_mixed.go(a_mixed)
    depth = 2 * cols
    early = jnp.dot(a_mixed.done, output_weight[:depth], preferred_element_type=F32)
    b_mixed.state, early = lax.optimization_barrier((b_mixed.state, early))
    b_mixed.go()
    outs = []
    wide = output_weight.shape[1] // CHUNKS
    for c in range(CHUNKS):
        at = slice(c * wide, (c + 1) * wide)
        part = early[:, at] + jnp.dot(
            b_mixed.done, output_weight[depth:, at], preferred_element_type=F32
        )
        outs.append((part[:own] + exchange(part[own:], 0, "yz")).astype(BF16))
    return jnp.concatenate(outs, 1)


def solution(mesh):
    return jax.shard_map(
        on_device,
        mesh=mesh,
        in_specs=(P(("groups", "yz"), "gx"), P("gx", "yz"), P("gx", None), P("yz", "gx")),
        out_specs=P(("groups", "yz"), "gx"),
        check_vma=False,
    )
```

time: 264 us -> 107 us (0.41)
  waiting for transfers between devices: 185 us -> 33.2 us
  starting transfers between devices: 0.12 us -> 36.6 us
  blocking collectives: 31.1 us -> 0 us
  between operations: 13.2 us -> 0.74 us
  local copies, waits for them, and re-layouts: 0.77 us -> 4.71 us
    reduce_scatter x2 -> x0, waiting for transfers between devices: 118 us -> none  [the longest x1 107 us: on_device(): lax.psum_scatter(jnp.concatenate([jnp.dot(whole, query_weight, preferred_...]
    all_gather x2 -> x0, waiting for transfers between devices: 66.4 us -> none  [the longest x1 52 us: on_device(): lax.all_gather(mixed, 'gx', axis=0, tiled=True)]
    ppermute x0 -> x29, starting transfers between devices: none -> 36.6 us  [exchange(): return lax.ppermute(x, axis, [(i, i ^ 1 << bit) for i in range(n)])]
    ppermute x0 -> x29, waiting for transfers between devices: none -> 33.2 us  [exchange(): return lax.ppermute(x, axis, [(i, i ^ 1 << bit) for i in range(n)])]
    all_gather x1 -> x0, blocking collectives: 31.1 us -> none  [on_device(): keyvalue = lax.all_gather(own_keys, 'gx', axis=0, tiled=True)]
    dot_general x4 -> x14, matrix products: 26.2 us -> 24.2 us  [the longest x8 12.2 us: product(): jnp.dot(rows.reshape(total // 2, -1), query_weight[:, first:first + cols]...]
  transfers between devices with their start and end apart: 4 -> 29, of which waited for: 4 -> 15; matrix products, arithmetic and copies ran while one was open for 0% -> 29% of each run, Pallas kernels for 0% -> 0%
where the time goes in v2:
time: 107 us; the launch traced here: 106 us
  starting transfers between devices  36.6 us (34%)
  waiting for transfers between devices  33.2 us (31%)
  matrix products  25.1 us (23%)
  other arithmetic  6.13 us (6%)
  local copies, waits for them, and re-layouts  4.71 us (4%)
    ppermute x29, starting transfers between devices, exchange(): return lax.ppermute(x, axis, [(i, i ^ 1 << bit) for i in range(n)])  36.6 us
    ppermute x29, waiting for transfers between devices, exchange(): return lax.ppermute(x, axis, [(i, i ^ 1 << bit) for i in range(n)])  33.2 us
    dot_general x8, matrix products, product(): jnp.dot(rows.reshape(total // 2, -1), query_weight[:, first:first + cols]...  12.2 us
    dot_general x1, matrix products, on_device(): jnp.dot(a_mixed.done, output_weight[:depth], preferred_element_type=F32)  5.56 us
    dot_general x2, matrix products, on_device(): jnp.dot(b_mixed.done, output_weight[depth:, at], preferred_element_type=F32)  3.44 us
    another operation x2, other arithmetic, on_device(): whole = jnp.stack([tokens, other]).reshape([2] + cube + [tokens.shape[1]])  2.77 us
    dot_general x1, matrix products, on_device(): jnp.dot(tokens, keyvalue_weight, preferred_element_type=F32)  2.54 us
    unnamed x17, local copies, waits for them, and re-layouts  2.26 us
  transfers between devices with their start and end apart: 29, of which 15 were waited for; matrix products, arithmetic and copies ran while one was open for 29% of the time, Pallas kernels for 0%

profile of v2, /device:TPU:0, one launch (start us, length us, event | category | flops | bytes accessed | tf_op | source)
XLA Modules:
  0.0 106.5 jit_solution(6713826158639456205)
XLA Ops:
  0.0 0.5 collective-permute-start.1
  0.5 1.2 %copy-done = bf16[2304,512]{1,0:T(8,128)(2,1)S(1)} copy-done((bf16[2304,512]{1,0:T(8,128)(2,1)S(1)}, bf16[2304,512]{1,0:T(8,128)(2,1)}, u32[]{:S(2)}) %copy-start) | copy-done | bytes 2359320
  1.7 2.5 %fusion.120 = f32[192,512]{1,0:T(8,128)} fusion(bf16[192,2304]{1,0:T(8,128)(2,1)} %param.4, bf16[2304,512]{1,0:T(8,128)(2,1)S(1)} %copy-done), kind=kOutput, calls=%fused_computation.197 | convolution fusion | flops 452984832 | bytes 3637248 | tf_op jit(solution)/shard_map/dot_general | solution.py:53
  4.2 1.0 dynamic-slice_bitcast_fusion
  5.3 3.0 %collective-permute-start = (f32[2,2,24,512]{3,2,1,0:T(8,128)S(1)}, f32[2,2,24,512]{3,2,1,0:T(8,128)S(1)}, u32[]{:S(2)}, u32[]{:S(2)}) collective-permute-start(f32[2,2,24,512]{3,2,1,0:T(8,128)S(1)} %get-tuple-element.225), channel_id=1, source_target_pairs={{0,2},{2,0},{4,6},{6,4},{8,10},{10,8},{12,14},{14,12},{1,3},{3,1},... | collective-permute-start | bytes 589832 | tf_op jit(solution)/shard_map/ppermute | solution.py:18
  8.6 1.5 %fusion.64 = (bf16[2,1,2,2,24,2304]{5,4,3,2,1,0:T(8,128)(2,1)S(1)}, bf16[2,1,2,2,24,2304]{5,4,3,2,1,0:T(8,128)(2,1)S(1)}) fusion(s32[]{:T(128)S(6)} %select_n.187, bf16[1,2,2,2,24,2304]{5,4,3,2,1,0:T(8,128)(2,1)S(1)} %bitcast.156, bf16[1,2,2,2,24,2304]{5,4,3,2,1,0:T(8,128)(2,1)} %bitcast.4, s32[]{:T(128)S(6)} %select_n.186), kind=kLoop, calls=%fused_computation.63 | loop fusion | flops 884736 | bytes 3538952 | tf_op jit(solution)/shard_map/stack | solution.py:69
  10.0 3.2 %fusion.41 = f16[192,768]{1,0:T(8,128)(2,1)S(1)} fusion(bf16[192,2304]{1,0:T(8,128)(2,1)S(1)} %bitcast.172, bf16[2304,3072]{1,0:T(8,128)(2,1)} %param.5), kind=kOutput, calls=%fused_computation.41 | convolution fusion | flops 679772160 | bytes 4718592 | tf_op jit(solution)/shard_map/dot_general | solution.py:75
  13.2 3.6 %fusion.47 = f16[192,768]{1,0:T(8,128)(2,1)S(1)} fusion(bf16[192,2304]{1,0:T(8,128)(2,1)S(1)} %bitcast.173, bf16[2304,3072]{1,0:T(8,128)(2,1)} %param.5), kind=kOutput, calls=%fused_computation.43 | convolution fusion | flops 679772160 | bytes 4718592 | tf_op jit(solution)/shard_map/dot_general | solution.py:75
  16.8 0.9 fusion.14
  17.8 0.9 fusion.22
  18.7 1.3 %fusion.61 = (bf16[2,2,1,2,24,2304]{5,4,3,2,1,0:T(8,128)(2,1)S(1)}, bf16[2,2,1,2,24,2304]{5,4,3,2,1,0:T(8,128)(2,1)S(1)}) fusion(s32[]{:T(128)S(6)} %select_n.189, bf16[1,2,2,2,24,2304]{5,4,3,2,1,0:T(8,128)(2,1)S(1)} %bitcast.157, bf16[1,2,2,2,24,2304]{5,4,3,2,1,0:T(8,128)(2,1)} %bitcast.4, s32[]{:T(128)S(6)} %select_n.188), kind=kLoop, calls=%fused_computation.60 | loop fusion | flops 884736 | bytes 3538952 | tf_op jit(solution)/shard_map/stack | solution.py:69
  20.0 0.9 fusion.38
  21.0 0.9 fusion.44
  22.0 2.0 %collective-permute-start.3 = (f16[192,768]{1,0:T(8,128)(2,1)S(1)}, f16[192,768]{1,0:T(8,128)(2,1)S(1)}, u32[]{:S(2)}, u32[]{:S(2)}) collective-permute-start(f16[192,768]{1,0:T(8,128)(2,1)S(1)} %fusion.44), channel_id=1, source_target_pairs={{0,4},{2,6},{4,0},{6,2},{8,12},{10,14},{12,8},{14,10},{1,5},{3,7},... | collective-permute-start | bytes 884744 | tf_op jit(solution)/shard_map/ppermute | solution.py:18
  24.1 0.9 fusion.10
  24.9 0.9 fusion.18
  25.8 1.6 %collective-permute-start.5 = (f16[192,768]{1,0:T(8,128)(2,1)S(1)}, f16[192,768]{1,0:T(8,128)(2,1)S(1)}, u32[]{:S(2)}, u32[]{:S(2)}) collective-permute-start(f16[192,768]{1,0:T(8,128)(2,1)S(1)} %fusion.41), channel_id=1, source_target_pairs={{0,2},{2,0},{4,6},{6,4},{8,10},{10,8},{12,14},{14,12},{1,3},{3,1},... | collective-permute-start | bytes 884744 | tf_op jit(solution)/shard_map/ppermute | solution.py:18
  27.4 0.4 collective-permute-start.6
  27.9 1.6 %collective-permute-start.4 = (f32[2,24,512]{2,1,0:T(8,128)S(1)}, f32[2,24,512]{2,1,0:T(8,128)S(1)}, u32[]{:S(2)}, u32[]{:S(2)}) collective-permute-start(f32[2,24,512]{2,1,0:T(8,128)S(1)} %get-tuple-element.245), channel_id=1, source_target_pairs={{0,4},{2,6},{4,0},{6,2},{8,12},{10,14},{12,8},{14,10},{1,5},{3,7},... | collective-permute-start | bytes 294920 | tf_op jit(solution)/shard_map/ppermute | solution.py:18
  29.6 2.3 %collective-permute-done.2 = f16[192,768]{1,0:T(8,128)(2,1)S(1)} collective-permute-done((f16[192,768]{1,0:T(8,128)(2,1)S(1)}, f16[192,768]{1,0:T(8,128)(2,1)S(1)}, u32[]{:S(2)}, u32[]{:S(2)}) %collective-permute-start.2) | collective-permute-done | bytes 294944 | tf_op jit(solution)/shard_map/ppermute | solution.py:18
  32.3 2.0 %collective-permute-start.9 = (f16[2,2,24,768]{3,2,0,1:T(8,128)(2,1)S(1)}, f16[2,2,24,768]{3,2,0,1:T(8,128)(2,1)S(1)}, u32[]{:S(2)}, u32[]{:S(2)}) collective-permute-start(f16[2,2,24,768]{3,2,0,1:T(8,128)(2,1)S(1)} %fusion.86), channel_id=1, source_target_pairs={{0,2},{2,0},{4,6},{6,4},{8,10},{10,8},{12,14},{14,12},{1,3},{3,1},... | collective-permute-start | bytes 442376 | tf_op jit(solution)/shard_map/ppermute | solution.py:18
  34.3 1.6 %collective-permute-start.8 = (f16[2,2,24,768]{3,2,0,1:T(8,128)(2,1)S(1)}, f16[2,2,24,768]{3,2,0,1:T(8,128)(2,1)S(1)}, u32[]{:S(2)}, u32[]{:S(2)}) collective-permute-start(f16[2,2,24,768]{3,2,0,1:T(8,128)(2,1)S(1)} %fusion.85), channel_id=1, source_target_pairs={{0,4},{2,6},{4,0},{6,2},{8,12},{10,14},{12,8},{14,10},{1,5},{3,7},... | collective-permute-start | bytes 442376 | tf_op jit(solution)/shard_map/ppermute | solution.py:18
  36.0 4.4 %collective-permute-done.4 = f32[2,24,512]{2,1,0:T(8,128)S(1)} collective-permute-done((f32[2,24,512]{2,1,0:T(8,128)S(1)}, f32[2,24,512]{2,1,0:T(8,128)S(1)}, u32[]{:S(2)}, u32[]{:S(2)}) %collective-permute-start.4) | collective-permute-done | bytes 98336 | tf_op jit(solution)/shard_map/ppermute | solution.py:18
  40.4 3.1 %collective-permute-start.7 = (f32[2,24,512]{2,1,0:T(8,128)S(1)}, f32[2,24,512]{2,1,0:T(8,128)S(1)}, u32[]{:S(2)}, u32[]{:S(2)}) collective-permute-start(f32[2,24,512]{2,1,0:T(8,128)S(1)} %add.169), channel_id=1, source_target_pairs={{0,8},{2,10},{4,12},{6,14},{8,0},{10,2},{12,4},{14,6},{1,9},{3,11}... | collective-permute-start | bytes 294920 | tf_op jit(solution)/shard_map/ppermute | solution.py:18
  43.7 1.6 %collective-permute-start.11 = (f16[2,2,24,768]{3,2,0,1:T(8,128)(2,1)S(1)}, f16[2,2,24,768]{3,2,0,1:T(8,128)(2,1)S(1)}, u32[]{:S(2)}, u32[]{:S(2)}) collective-permute-start(f16[2,2,24,768]{3,2,0,1:T(8,128)(2,1)S(1)} %fusion.87), channel_id=1, source_target_pairs={{0,4},{2,6},{4,0},{6,2},{8,12},{10,14},{12,8},{14,10},{1,5},{3,7},... | collective-permute-start | bytes 442376 | tf_op jit(solution)/shard_map/ppermute | solution.py:18
  45.5 1.6 %collective-permute-start.12 = (f16[2,2,24,768]{3,2,0,1:T(8,128)(2,1)S(1)}, f16[2,2,24,768]{3,2,0,1:T(8,128)(2,1)S(1)}, u32[]{:S(2)}, u32[]{:S(2)}) collective-permute-start(f16[2,2,24,768]{3,2,0,1:T(8,128)(2,1)S(1)} %fusion.88), channel_id=1, source_target_pairs={{0,2},{2,0},{4,6},{6,4},{8,10},{10,8},{12,14},{14,12},{1,3},{3,1},... | collective-permute-start | bytes 442376 | tf_op jit(solution)/shard_map/ppermute | solution.py:18
  47.2 1.6 %collective-permute-start.10 = (bf16[2,24,512]{2,1,0:T(8,128)(2,1)S(1)}, bf16[2,24,512]{2,1,0:T(8,128)(2,1)S(1)}, u32[]{:S(2)}, u32[]{:S(2)}) collective-permute-start(bf16[2,24,512]{2,1,0:T(8,128)(2,1)S(1)} %add_convert_fusion.2), channel_id=1, source_target_pairs={{0,4},{2,6},{4,0},{6,2},{8,12},{10,14},{12,8},{14,10},{1,5},{3,7},... | collective-permute-start | bytes 147464 | tf_op jit(solution)/shard_map/ppermute | solution.py:18
  49.0 3.3 %collective-permute-start.14 = (f16[2,24,1536]{2,1,0:T(8,128)(2,1)S(1)}, f16[2,24,1536]{2,1,0:T(8,128)(2,1)S(1)}, u32[]{:S(2)}, u32[]{:S(2)}) collective-permute-start(f16[2,24,1536]{2,1,0:T(8,128)(2,1)S(1)} %get-tuple-element.215), channel_id=1, source_target_pairs={{0,8},{2,10},{4,12},{6,14},{8,0},{10,2},{12,4},{14,6},{1,9},{3,11}... | collective-permute-start | bytes 442376 | tf_op jit(solution)/shard_map/ppermute | solution.py:18
  52.3 1.6 %collective-permute-start.13 = (bf16[2,2,24,512]{3,2,1,0:T(8,128)(2,1)S(1)}, bf16[2,2,24,512]{3,2,1,0:T(8,128)(2,1)S(1)}, u32[]{:S(2)}, u32[]{:S(2)}) collective-permute-start(bf16[2,2,24,512]{3,2,1,0:T(8,128)(2,1)S(1)} %pad_maximum_fusion.19), channel_id=1, source_target_pairs={{0,2},{2,0},{4,6},{6,4},{8,10},{10,8},{12,14},{14,12},{1,3},{3,1},... | collective-permute-start | bytes 294920 | tf_op jit(solution)/shard_map/ppermute | solution.py:18
  54.0 1.9 %collective-permute-start.16 = (f16[2,24,1536]{2,1,0:T(8,128)(2,1)S(1)}, f16[2,24,1536]{2,1,0:T(8,128)(2,1)S(1)}, u32[]{:S(2)}, u32[]{:S(2)}) collective-permute-start(f16[2,24,1536]{2,1,0:T(8,128)(2,1)S(1)} %get-tuple-element.213), channel_id=1, source_target_pairs={{0,8},{2,10},{4,12},{6,14},{8,0},{10,2},{12,4},{14,6},{1,9},{3,11}... | collective-permute-start | bytes 442376 | tf_op jit(solution)/shard_map/ppermute | solution.py:18
  55.9 1.0 collective-permute-done.13
  57.1 1.2 %collective-permute-done.14 = f16[2,24,1536]{2,1,0:T(8,128)(2,1)S(1)} collective-permute-done((f16[2,24,1536]{2,1,0:T(8,128)(2,1)S(1)}, f16[2,24,1536]{2,1,0:T(8,128)(2,1)S(1)}, u32[]{:S(2)}, u32[]{:S(2)}) %collective-permute-start.14) | collective-permute-done | bytes 147488 | tf_op jit(solution)/shard_map/ppermute | solution.py:18
  58.3 0.2 reshape.161
  58.6 0.4 fusion.114
  59.2 0.2 fusion.59
  59.5 0.2 reshape.162
  59.6 1.9 %collective-permute-start.17 = (bf16[2,24,1536]{2,1,0:T(8,128)(2,1)S(1)}, bf16[2,24,1536]{2,1,0:T(8,128)(2,1)S(1)}, u32[]{:S(2)}, u32[]{:S(2)}) collective-permute-start(bf16[2,24,1536]{2,1,0:T(8,128)(2,1)S(1)} %reshape.162), channel_id=1, source_target_pairs={{0,8},{2,10},{4,12},{6,14},{8,0},{10,2},{12,4},{14,6},{1,9},{3,11}... | collective-permute-start | bytes 442376 | tf_op jit(solution)/shard_map/ppermute | solution.py:18
  61.6 0.2 collective-permute-done.16
  61.8 0.2 reshape.163
  61.9 0.4 fusion.117
  62.5 0.2 fusion.60
  62.8 0.2 reshape.164
  63.0 1.0 collective-permute-start.18
  64.0 9.6 %collective-permute-done.17 = bf16[2,24,1536]{2,1,0:T(8,128)(2,1)S(1)} collective-permute-done((bf16[2,24,1536]{2,1,0:T(8,128)(2,1)S(1)}, bf16[2,24,1536]{2,1,0:T(8,128)(2,1)S(1)}, u32[]{:S(2)}, u32[]{:S(2)}) %collective-permute-start.17) | collective-permute-done | bytes 147488 | tf_op jit(solution)/shard_map/ppermute | solution.py:18
  73.6 1.7 %collective-permute-start.20 = (bf16[2,2,24,768]{3,2,0,1:T(8,128)(2,1)S(1)}, bf16[2,2,24,768]{3,2,0,1:T(8,128)(2,1)S(1)}, u32[]{:S(2)}, u32[]{:S(2)}) collective-permute-start(bf16[2,2,24,768]{3,2,0,1:T(8,128)(2,1)S(1)} %get-tuple-element.178), channel_id=1, source_target_pairs={{0,2},{2,0},{4,6},{6,4},{8,10},{10,8},{12,14},{14,12},{1,3},{3,1},... | collective-permute-start | bytes 442376 | tf_op jit(solution)/shard_map/ppermute | solution.py:18
  75.3 0.7 collective-permute-done.18
  76.0 1.7 %collective-permute-start.22 = (bf16[2,2,24,768]{3,2,0,1:T(8,128)(2,1)S(1)}, bf16[2,2,24,768]{3,2,0,1:T(8,128)(2,1)S(1)}, u32[]{:S(2)}, u32[]{:S(2)}) collective-permute-start(bf16[2,2,24,768]{3,2,0,1:T(8,128)(2,1)S(1)} %get-tuple-element.184), channel_id=1, source_target_pairs={{0,2},{2,0},{4,6},{6,4},{8,10},{10,8},{12,14},{14,12},{1,3},{3,1},... | collective-permute-start | bytes 442376 | tf_op jit(solution)/shard_map/ppermute | solution.py:18
  77.7 0.2 collective-permute-start.21
  77.9 1.7 %collective-permute-done.20 = bf16[2,2,24,768]{3,2,0,1:T(8,128)(2,1)S(1)} collective-permute-done((bf16[2,2,24,768]{3,2,0,1:T(8,128)(2,1)S(1)}, bf16[2,2,24,768]{3,2,0,1:T(8,128)(2,1)S(1)}, u32[]{:S(2)}, u32[]{:S(2)}) %collective-permute-start.20) | collective-permute-done | bytes 147488 | tf_op jit(solution)/shard_map/ppermute | solution.py:18
  79.6 2.1 %collective-permute-done.19 = bf16[2,2,24,768]{3,2,0,1:T(8,128)(2,1)S(1)} collective-permute-done((bf16[2,2,24,768]{3,2,0,1:T(8,128)(2,1)S(1)}, bf16[2,2,24,768]{3,2,0,1:T(8,128)(2,1)S(1)}, u32[]{:S(2)}, u32[]{:S(2)}) %collective-permute-start.19) | collective-permute-done | bytes 147488 | tf_op jit(solution)/shard_map/ppermute | solution.py:18
  81.9 0.2 pad_maximum_fusion.12
  82.1 0.3 collective-permute-start.23
  82.4 0.3 collective-permute-done.22
  82.7 2.2 %collective-permute-done.21 = bf16[2,2,24,768]{3,2,0,1:T(8,128)(2,1)S(1)} collective-permute-done((bf16[2,2,24,768]{3,2,0,1:T(8,128)(2,1)S(1)}, bf16[2,2,24,768]{3,2,0,1:T(8,128)(2,1)S(1)}, u32[]{:S(2)}, u32[]{:S(2)}) %collective-permute-start.21) | collective-permute-done | bytes 147488 | tf_op jit(solution)/shard_map/ppermute | solution.py:18
  85.1 1.4 %collective-permute-start.25 = (bf16[2,2,2,24,768]{4,3,0,2,1:T(8,128)(2,1)S(1)}, bf16[2,2,2,24,768]{4,3,0,2,1:T(8,128)(2,1)S(1)}, u32[]{:S(2)}, u32[]{:S(2)}) collective-permute-start(bf16[2,2,2,24,768]{4,3,0,2,1:T(8,128)(2,1)S(1)} %pad_maximum_fusion.14), channel_id=1, source_target_pairs={{0,2},{2,0},{4,6},{6,4},{8,10},{10,8},{12,14},{14,12},{1,3},{3,1},... | collective-permute-start | bytes 884744 | tf_op jit(solution)/shard_map/ppermute | solution.py:18
  86.5 5.3 %collective-permute-done.24 = bf16[2,2,2,24,768]{4,3,0,2,1:T(8,128)(2,1)S(1)} collective-permute-done((bf16[2,2,2,24,768]{4,3,0,2,1:T(8,128)(2,1)S(1)}, bf16[2,2,2,24,768]{4,3,0,2,1:T(8,128)(2,1)S(1)}, u32[]{:S(2)}, u32[]{:S(2)}) %collective-permute-start.24) | collective-permute-done | bytes 294944 | tf_op jit(solution)/shard_map/ppermute | solution.py:18
  92.2 5.6 %fusion.2 = f32[384,2304]{1,0:T(8,128)S(1)} fusion(bf16[3072,2304]{1,0:T(8,128)(2,1)} %param.7, bf16[384,768]{1,0:T(8,128)(2,1)S(1)} %bitcast.181, bf16[384,768]{1,0:T(8,128)(2,1)S(1)} %bitcast.178), kind=kOutput, calls=%fused_computation.2 | convolution fusion | flops 2720268288 | bytes 11796480 | tf_op jit(solution)/shard_map/dot_general | solution.py:163
  98.1 0.6 slice-done.2
  98.7 0.4 slice-done.3
  99.1 1.7 %slice_add_fusion = f32[384,1152]{1,0:T(8,128)S(1)} fusion(f32[384,2304]{1,0:T(8,128)S(1)} %fusion.2, bf16[3072,2304]{1,0:T(8,128)(2,1)S(1)} %bitcast.184, bf16[384,768]{1,0:T(8,128)(2,1)S(1)} %bitcast.179, bf16[384,768]{1,0:T(8,128)(2,1)S(1)} %bitcast.176), kind=kOutput, calls=%fused_computation.32 | convolution fusion | flops 1361756160 | bytes 8257536 | tf_op jit(solution)/shard_map/dot_general | solution.py:170
  101.0 1.7 %slice_add_fusion.1 = f32[384,1152]{1,0:T(8,128)S(1)} fusion(f32[384,2304]{1,0:T(8,128)S(1)} %fusion.2, bf16[3072,2304]{1,0:T(8,128)(2,1)S(1)} %bitcast.184, bf16[384,768]{1,0:T(8,128)(2,1)S(1)} %bitcast.180, bf16[384,768]{1,0:T(8,128)(2,1)S(1)} %bitcast.177), kind=kOutput, calls=%fused_computation.33 | convolution fusion | flops 1361756160 | bytes 8257536 | tf_op jit(solution)/shard_map/dot_general | solution.py:170
  102.8 0.6 collective-permute-start.27
  103.5 1.9 %collective-permute-done.27 = f32[192,1152]{1,0:T(8,128)S(1)} collective-permute-done((f32[192,1152]{1,0:T(8,128)S(1)}, f32[192,1152]{1,0:T(8,128)S(1)}, u32[]{:S(2)}, u32[]{:S(2)}) %collective-permute-start.27) | collective-permute-done | bytes 884768 | tf_op jit(solution)/shard_map/ppermute | solution.py:18
  105.5 1.0 pad_maximum_fusion.1
  (105 shorter events, 3.5 us)
Async XLA Ops:
  0.0 1.7 %copy-start = (bf16[2304,512]{1,0:T(8,128)(2,1)S(1)}, bf16[2304,512]{1,0:T(8,128)(2,1)}, u32[]{:S(2)}) copy-start(bf16[2304,512]{1,0:T(8,128)(2,1)} %param.6) | copy-start | bytes 7077892
  0.0 8.6 %copy-start.2 = (bf16[192,2304]{1,0:T(8,128)(2,1)S(1)}, bf16[192,2304]{1,0:T(8,128)(2,1)}, u32[]{:S(2)}) copy-start(bf16[192,2304]{1,0:T(8,128)(2,1)} %param.4) | copy-start | bytes 2654212
  0.0 8.5 %collective-permute-start.1 = (bf16[192,2304]{1,0:T(8,128)(2,1)}, bf16[192,2304]{1,0:T(8,128)(2,1)}, u32[]{:S(2)}, u32[]{:S(2)}) collective-permute-start(bf16[192,2304]{1,0:T(8,128)(2,1)} %param.4), channel_id=1, source_target_pairs={{0,1},{1,0},{2,3},{3,2},{4,5},{5,4},{6,7},{7,6},{8,9},{9,8},{10,11... | collective-permute-start | bytes 2654216 | tf_op jit(solution)/shard_map/ppermute | solution.py:18
  5.3 22.6 %collective-permute-start = (f32[2,2,24,512]{3,2,1,0:T(8,128)S(1)}, f32[2,2,24,512]{3,2,1,0:T(8,128)S(1)}, u32[]{:S(2)}, u32[]{:S(2)}) collective-permute-start(f32[2,2,24,512]{3,2,1,0:T(8,128)S(1)} %get-tuple-element.225), channel_id=1, source_target_pairs={{0,2},{2,0},{4,6},{6,4},{8,10},{10,8},{12,14},{14,12},{1,3},{3,1},... | collective-permute-start | bytes 589832 | tf_op jit(solution)/shard_map/ppermute | solution.py:18
  8.6 8.3 %copy-start.3 = (bf16[2304,3072]{1,0:T(8,128)(2,1)S(1)}, bf16[2304,3072]{1,0:T(8,128)(2,1)}, u32[]{:S(2)}) copy-start(bf16[2304,3072]{1,0:T(8,128)(2,1)} %param.5) | copy-start | bytes 42467332
  21.9 10.0 %collective-permute-start.2 = (f16[192,768]{1,0:T(8,128)(2,1)S(1)}, f16[192,768]{1,0:T(8,128)(2,1)S(1)}, u32[]{:S(2)}, u32[]{:S(2)}) collective-permute-start(f16[192,768]{1,0:T(8,128)(2,1)S(1)} %fusion.47), channel_id=1, source_target_pairs={{0,2},{2,0},{4,6},{6,4},{8,10},{10,8},{12,14},{14,12},{1,3},{3,1},... | collective-permute-start | bytes 884744 | tf_op jit(solution)/shard_map/ppermute | solution.py:18
  22.0 10.0 %collective-permute-start.3 = (f16[192,768]{1,0:T(8,128)(2,1)S(1)}, f16[192,768]{1,0:T(8,128)(2,1)S(1)}, u32[]{:S(2)}, u32[]{:S(2)}) collective-permute-start(f16[192,768]{1,0:T(8,128)(2,1)S(1)} %fusion.44), channel_id=1, source_target_pairs={{0,4},{2,6},{4,0},{6,2},{8,12},{10,14},{12,8},{14,10},{1,5},{3,7},... | collective-permute-start | bytes 884744 | tf_op jit(solution)/shard_map/ppermute | solution.py:18
  25.8 17.7 %collective-permute-start.5 = (f16[192,768]{1,0:T(8,128)(2,1)S(1)}, f16[192,768]{1,0:T(8,128)(2,1)S(1)}, u32[]{:S(2)}, u32[]{:S(2)}) collective-permute-start(f16[192,768]{1,0:T(8,128)(2,1)S(1)} %fusion.41), channel_id=1, source_target_pairs={{0,2},{2,0},{4,6},{6,4},{8,10},{10,8},{12,14},{14,12},{1,3},{3,1},... | collective-permute-start | bytes 884744 | tf_op jit(solution)/shard_map/ppermute | solution.py:18
  27.4 16.1 %collective-permute-start.6 = (f16[192,768]{1,0:T(8,128)(2,1)S(1)}, f16[192,768]{1,0:T(8,128)(2,1)S(1)}, u32[]{:S(2)}, u32[]{:S(2)}) collective-permute-start(f16[192,768]{1,0:T(8,128)(2,1)S(1)} %fusion.38), channel_id=1, source_target_pairs={{0,4},{2,6},{4,0},{6,2},{8,12},{10,14},{12,8},{14,10},{1,5},{3,7},... | collective-permute-start | bytes 884744 | tf_op jit(solution)/shard_map/ppermute | solution.py:18
  27.9 12.5 %collective-permute-start.4 = (f32[2,24,512]{2,1,0:T(8,128)S(1)}, f32[2,24,512]{2,1,0:T(8,128)S(1)}, u32[]{:S(2)}, u32[]{:S(2)}) collective-permute-start(f32[2,24,512]{2,1,0:T(8,128)S(1)} %get-tuple-element.245), channel_id=1, source_target_pairs={{0,4},{2,6},{4,0},{6,2},{8,12},{10,14},{12,8},{14,10},{1,5},{3,7},... | collective-permute-start | bytes 294920 | tf_op jit(solution)/shard_map/ppermute | solution.py:18
  32.3 16.5 %collective-permute-start.9 = (f16[2,2,24,768]{3,2,0,1:T(8,128)(2,1)S(1)}, f16[2,2,24,768]{3,2,0,1:T(8,128)(2,1)S(1)}, u32[]{:S(2)}, u32[]{:S(2)}) collective-permute-start(f16[2,2,24,768]{3,2,0,1:T(8,128)(2,1)S(1)} %fusion.86), channel_id=1, source_target_pairs={{0,2},{2,0},{4,6},{6,4},{8,10},{10,8},{12,14},{14,12},{1,3},{3,1},... | collective-permute-start | bytes 442376 | tf_op jit(solution)/shard_map/ppermute | solution.py:18
  34.3 14.5 %collective-permute-start.8 = (f16[2,2,24,768]{3,2,0,1:T(8,128)(2,1)S(1)}, f16[2,2,24,768]{3,2,0,1:T(8,128)(2,1)S(1)}, u32[]{:S(2)}, u32[]{:S(2)}) collective-permute-start(f16[2,2,24,768]{3,2,0,1:T(8,128)(2,1)S(1)} %fusion.85), channel_id=1, source_target_pairs={{0,4},{2,6},{4,0},{6,2},{8,12},{10,14},{12,8},{14,10},{1,5},{3,7},... | collective-permute-start | bytes 442376 | tf_op jit(solution)/shard_map/ppermute | solution.py:18
  40.4 6.7 %collective-permute-start.7 = (f32[2,24,512]{2,1,0:T(8,128)S(1)}, f32[2,24,512]{2,1,0:T(8,128)S(1)}, u32[]{:S(2)}, u32[]{:S(2)}) collective-permute-start(f32[2,24,512]{2,1,0:T(8,128)S(1)} %add.169), channel_id=1, source_target_pairs={{0,8},{2,10},{4,12},{6,14},{8,0},{10,2},{12,4},{14,6},{1,9},{3,11}... | collective-permute-start | bytes 294920 | tf_op jit(solution)/shard_map/ppermute | solution.py:18
  43.7 10.2 %collective-permute-start.11 = (f16[2,2,24,768]{3,2,0,1:T(8,128)(2,1)S(1)}, f16[2,2,24,768]{3,2,0,1:T(8,128)(2,1)S(1)}, u32[]{:S(2)}, u32[]{:S(2)}) collective-permute-start(f16[2,2,24,768]{3,2,0,1:T(8,128)(2,1)S(1)} %fusion.87), channel_id=1, source_target_pairs={{0,4},{2,6},{4,0},{6,2},{8,12},{10,14},{12,8},{14,10},{1,5},{3,7},... | collective-permute-start | bytes 442376 | tf_op jit(solution)/shard_map/ppermute | solution.py:18
  45.5 8.3 %collective-permute-start.12 = (f16[2,2,24,768]{3,2,0,1:T(8,128)(2,1)S(1)}, f16[2,2,24,768]{3,2,0,1:T(8,128)(2,1)S(1)}, u32[]{:S(2)}, u32[]{:S(2)}) collective-permute-start(f16[2,2,24,768]{3,2,0,1:T(8,128)(2,1)S(1)} %fusion.88), channel_id=1, source_target_pairs={{0,2},{2,0},{4,6},{6,4},{8,10},{10,8},{12,14},{14,12},{1,3},{3,1},... | collective-permute-start | bytes 442376 | tf_op jit(solution)/shard_map/ppermute | solution.py:18
  47.2 5.1 %collective-permute-start.10 = (bf16[2,24,512]{2,1,0:T(8,128)(2,1)S(1)}, bf16[2,24,512]{2,1,0:T(8,128)(2,1)S(1)}, u32[]{:S(2)}, u32[]{:S(2)}) collective-permute-start(bf16[2,24,512]{2,1,0:T(8,128)(2,1)S(1)} %add_convert_fusion.2), channel_id=1, source_target_pairs={{0,4},{2,6},{4,0},{6,2},{8,12},{10,14},{12,8},{14,10},{1,5},{3,7},... | collective-permute-start | bytes 147464 | tf_op jit(solution)/shard_map/ppermute | solution.py:18
  49.0 9.4 %collective-permute-start.14 = (f16[2,24,1536]{2,1,0:T(8,128)(2,1)S(1)}, f16[2,24,1536]{2,1,0:T(8,128)(2,1)S(1)}, u32[]{:S(2)}, u32[]{:S(2)}) collective-permute-start(f16[2,24,1536]{2,1,0:T(8,128)(2,1)S(1)} %get-tuple-element.215), channel_id=1, source_target_pairs={{0,8},{2,10},{4,12},{6,14},{8,0},{10,2},{12,4},{14,6},{1,9},{3,11}... | collective-permute-start | bytes 442376 | tf_op jit(solution)/shard_map/ppermute | solution.py:18
  52.3 4.7 %collective-permute-start.13 = (bf16[2,2,24,512]{3,2,1,0:T(8,128)(2,1)S(1)}, bf16[2,2,24,512]{3,2,1,0:T(8,128)(2,1)S(1)}, u32[]{:S(2)}, u32[]{:S(2)}) collective-permute-start(bf16[2,2,24,512]{3,2,1,0:T(8,128)(2,1)S(1)} %pad_maximum_fusion.19), channel_id=1, source_target_pairs={{0,2},{2,0},{4,6},{6,4},{8,10},{10,8},{12,14},{14,12},{1,3},{3,1},... | collective-permute-start | bytes 294920 | tf_op jit(solution)/shard_map/ppermute | solution.py:18
  54.0 7.7 %collective-permute-start.16 = (f16[2,24,1536]{2,1,0:T(8,128)(2,1)S(1)}, f16[2,24,1536]{2,1,0:T(8,128)(2,1)S(1)}, u32[]{:S(2)}, u32[]{:S(2)}) collective-permute-start(f16[2,24,1536]{2,1,0:T(8,128)(2,1)S(1)} %get-tuple-element.213), channel_id=1, source_target_pairs={{0,8},{2,10},{4,12},{6,14},{8,0},{10,2},{12,4},{14,6},{1,9},{3,11}... | collective-permute-start | bytes 442376 | tf_op jit(solution)/shard_map/ppermute | solution.py:18
  57.0 1.5 %collective-permute-start.15 = (bf16[192,512]{1,0:T(8,128)(2,1)S(1)}, bf16[192,512]{1,0:T(8,128)(2,1)S(1)}, u32[]{:S(2)}, u32[]{:S(2)}) collective-permute-start(bf16[192,512]{1,0:T(8,128)(2,1)S(1)} %bitcast.174), channel_id=1, source_target_pairs={{0,1},{1,0},{2,3},{3,2},{4,5},{5,4},{6,7},{7,6},{8,9},{9,8},{10,11... | collective-permute-start | bytes 589832 | tf_op jit(solution)/shard_map/ppermute | solution.py:18
  59.6 13.9 %collective-permute-start.17 = (bf16[2,24,1536]{2,1,0:T(8,128)(2,1)S(1)}, bf16[2,24,1536]{2,1,0:T(8,128)(2,1)S(1)}, u32[]{:S(2)}, u32[]{:S(2)}) collective-permute-start(bf16[2,24,1536]{2,1,0:T(8,128)(2,1)S(1)} %reshape.162), channel_id=1, source_target_pairs={{0,8},{2,10},{4,12},{6,14},{8,0},{10,2},{12,4},{14,6},{1,9},{3,11}... | collective-permute-start | bytes 442376 | tf_op jit(solution)/shard_map/ppermute | solution.py:18
  63.0 13.0 %collective-permute-start.18 = (bf16[2,24,1536]{2,1,0:T(8,128)(2,1)S(1)}, bf16[2,24,1536]{2,1,0:T(8,128)(2,1)S(1)}, u32[]{:S(2)}, u32[]{:S(2)}) collective-permute-start(bf16[2,24,1536]{2,1,0:T(8,128)(2,1)S(1)} %reshape.164), channel_id=1, source_target_pairs={{0,8},{2,10},{4,12},{6,14},{8,0},{10,2},{12,4},{14,6},{1,9},{3,11}... | collective-permute-start | bytes 442376 | tf_op jit(solution)/shard_map/ppermute | solution.py:18
  73.6 6.0 %collective-permute-start.20 = (bf16[2,2,24,768]{3,2,0,1:T(8,128)(2,1)S(1)}, bf16[2,2,24,768]{3,2,0,1:T(8,128)(2,1)S(1)}, u32[]{:S(2)}, u32[]{:S(2)}) collective-permute-start(bf16[2,2,24,768]{3,2,0,1:T(8,128)(2,1)S(1)} %get-tuple-element.178), channel_id=1, source_target_pairs={{0,2},{2,0},{4,6},{6,4},{8,10},{10,8},{12,14},{14,12},{1,3},{3,1},... | collective-permute-start | bytes 442376 | tf_op jit(solution)/shard_map/ppermute | solution.py:18
  75.3 6.5 %collective-permute-start.19 = (bf16[2,2,24,768]{3,2,0,1:T(8,128)(2,1)S(1)}, bf16[2,2,24,768]{3,2,0,1:T(8,128)(2,1)S(1)}, u32[]{:S(2)}, u32[]{:S(2)}) collective-permute-start(bf16[2,2,24,768]{3,2,0,1:T(8,128)(2,1)S(1)} %get-tuple-element.176), channel_id=1, source_target_pairs={{0,4},{2,6},{4,0},{6,2},{8,12},{10,14},{12,8},{14,10},{1,5},{3,7},... | collective-permute-start | bytes 442376 | tf_op jit(solution)/shard_map/ppermute | solution.py:18
  76.0 6.7 %collective-permute-start.22 = (bf16[2,2,24,768]{3,2,0,1:T(8,128)(2,1)S(1)}, bf16[2,2,24,768]{3,2,0,1:T(8,128)(2,1)S(1)}, u32[]{:S(2)}, u32[]{:S(2)}) collective-permute-start(bf16[2,2,24,768]{3,2,0,1:T(8,128)(2,1)S(1)} %get-tuple-element.184), channel_id=1, source_target_pairs={{0,2},{2,0},{4,6},{6,4},{8,10},{10,8},{12,14},{14,12},{1,3},{3,1},... | collective-permute-start | bytes 442376 | tf_op jit(solution)/shard_map/ppermute | solution.py:18
  77.7 7.2 %collective-permute-start.21 = (bf16[2,2,24,768]{3,2,0,1:T(8,128)(2,1)S(1)}, bf16[2,2,24,768]{3,2,0,1:T(8,128)(2,1)S(1)}, u32[]{:S(2)}, u32[]{:S(2)}) collective-permute-start(bf16[2,2,24,768]{3,2,0,1:T(8,128)(2,1)S(1)} %get-tuple-element.182), channel_id=1, source_target_pairs={{0,4},{2,6},{4,0},{6,2},{8,12},{10,14},{12,8},{14,10},{1,5},{3,7},... | collective-permute-start | bytes 442376 | tf_op jit(solution)/shard_map/ppermute | solution.py:18
  81.8 10.0 %collective-permute-start.24 = (bf16[2,2,2,24,768]{4,3,0,2,1:T(8,128)(2,1)S(1)}, bf16[2,2,2,24,768]{4,3,0,2,1:T(8,128)(2,1)S(1)}, u32[]{:S(2)}, u32[]{:S(2)}) collective-permute-start(bf16[2,2,2,24,768]{4,3,0,2,1:T(8,128)(2,1)S(1)} %pad_maximum_fusion.13), channel_id=1, source_target_pairs={{0,4},{2,6},{4,0},{6,2},{8,12},{10,14},{12,8},{14,10},{1,5},{3,7},... | collective-permute-start | bytes 884744 | tf_op jit(solution)/shard_map/ppermute | solution.py:18
  82.1 9.7 %collective-permute-start.23 = (bf16[2,2,2,24,768]{4,3,0,2,1:T(8,128)(2,1)S(1)}, bf16[2,2,2,24,768]{4,3,0,2,1:T(8,128)(2,1)S(1)}, u32[]{:S(2)}, u32[]{:S(2)}) collective-permute-start(bf16[2,2,2,24,768]{4,3,0,2,1:T(8,128)(2,1)S(1)} %pad_maximum_fusion.12), channel_id=1, source_target_pairs={{0,2},{2,0},{4,6},{6,4},{8,10},{10,8},{12,14},{14,12},{1,3},{3,1},... | collective-permute-start | bytes 884744 | tf_op jit(solution)/shard_map/ppermute | solution.py:18
  85.0 12.8 %collective-permute-start.26 = (bf16[2,2,2,24,768]{4,3,0,2,1:T(8,128)(2,1)S(1)}, bf16[2,2,2,24,768]{4,3,0,2,1:T(8,128)(2,1)S(1)}, u32[]{:S(2)}, u32[]{:S(2)}) collective-permute-start(bf16[2,2,2,24,768]{4,3,0,2,1:T(8,128)(2,1)S(1)} %pad_maximum_fusion.15), channel_id=1, source_target_pairs={{0,4},{2,6},{4,0},{6,2},{8,12},{10,14},{12,8},{14,10},{1,5},{3,7},... | collective-permute-start | bytes 884744 | tf_op jit(solution)/shard_map/ppermute | solution.py:18
  85.1 12.7 %collective-permute-start.25 = (bf16[2,2,2,24,768]{4,3,0,2,1:T(8,128)(2,1)S(1)}, bf16[2,2,2,24,768]{4,3,0,2,1:T(8,128)(2,1)S(1)}, u32[]{:S(2)}, u32[]{:S(2)}) collective-permute-start(bf16[2,2,2,24,768]{4,3,0,2,1:T(8,128)(2,1)S(1)} %pad_maximum_fusion.14), channel_id=1, source_target_pairs={{0,2},{2,0},{4,6},{6,4},{8,10},{10,8},{12,14},{14,12},{1,3},{3,1},... | collective-permute-start | bytes 884744 | tf_op jit(solution)/shard_map/ppermute | solution.py:18
  91.9 6.2 %slice-start = ((s8[14155776]{0:T(1024)(128)(4,1)}), s8[4194304]{0:T(1024)(128)(4,1)S(1)}, s32[]{:S(2)}) async-start(s8[14155776]{0:T(1024)(128)(4,1)} %bitcast.183), calls=%async_computation | async-start | bytes 8388608
  92.2 6.0 %slice-start.1 = ((s8[14155776]{0:T(1024)(128)(4,1)}), s8[4194304]{0:T(1024)(128)(4,1)S(1)}, s32[]{:S(2)}) async-start(s8[14155776]{0:T(1024)(128)(4,1)} %bitcast.183), calls=%async_computation.1 | async-start | bytes 8388608
  92.2 6.6 %slice-start.2 = ((s8[14155776]{0:T(1024)(128)(4,1)}), s8[4194304]{0:T(1024)(128)(4,1)S(1)}, s32[]{:S(2)}) async-start(s8[14155776]{0:T(1024)(128)(4,1)} %bitcast.183), calls=%async_computation.2 | async-start | bytes 8388608
  92.2 6.9 %slice-start.3 = ((s8[14155776]{0:T(1024)(128)(4,1)}), s8[1572864]{0:T(1024)(128)(4,1)S(1)}, s32[]{:S(2)}) async-start(s8[14155776]{0:T(1024)(128)(4,1)} %bitcast.183), calls=%async_computation.3 | async-start | bytes 3145728
  100.9 2.5 %collective-permute-start.28 = (f32[192,1152]{1,0:T(8,128)S(1)}, f32[192,1152]{1,0:T(8,128)S(1)}, u32[]{:S(2)}, u32[]{:S(2)}) collective-permute-start(f32[192,1152]{1,0:T(8,128)S(1)} %slice.91), channel_id=1, source_target_pairs={{0,1},{1,0},{2,3},{3,2},{4,5},{5,4},{6,7},{7,6},{8,9},{9,8},{10,11... | collective-permute-start | bytes 2654216 | tf_op jit(solution)/shard_map/ppermute | solution.py:18
  102.7 3.8 %copy-start.1 = (bf16[2304,512]{1,0:T(8,128)(2,1)S(1)}, bf16[2304,512]{1,0:T(8,128)(2,1)}, u32[]{:S(2)}) copy-start(bf16[2304,512]{1,0:T(8,128)(2,1)} %param.6) | copy-start | bytes 7077892
  102.8 2.6 %collective-permute-start.27 = (f32[192,1152]{1,0:T(8,128)S(1)}, f32[192,1152]{1,0:T(8,128)S(1)}, u32[]{:S(2)}, u32[]{:S(2)}) collective-permute-start(f32[192,1152]{1,0:T(8,128)S(1)} %slice.89), channel_id=1, source_target_pairs={{0,1},{1,0},{2,3},{3,2},{4,5},{5,4},{6,7},{7,6},{8,9},{9,8},{10,11... | collective-permute-start | bytes 2654216 | tf_op jit(solution)/shard_map/ppermute | solution.py:18

commit v3 on v2

v3 whole, which is shorter than its diff:
```python
import jax
import jax.numpy as jnp
from jax import lax
from jax.sharding import PartitionSpec as P

HEAD = 256
PROMPTS = 1
GROUPS = 2
F32 = jnp.float32
BF16 = jnp.bfloat16
F16 = jnp.float16
SCALE = 0.5


def to_other_core(x):
    return lax.ppermute(x, "yz", [(0, 1), (1, 0)])


def pick(x, at, axis):
    return lax.dynamic_index_in_dim(x, at, axis, keepdims=False)


def half(x):
    return (x * SCALE).astype(F16)


def full(x):
    return x.astype(F32) * (1.0 / SCALE)


def after(x, *made):
    return lax.optimization_barrier((x, made))[0]


def on_device(tokens, query_weight, keyvalue_weight, output_weight):
    n = lax.axis_size("gx")
    m = n.bit_length() - 1
    core = lax.axis_index("yz")
    place = lax.axis_index("gx")
    own = tokens.shape[0]
    total = 2 * own
    small = own // n
    span = 2 * small
    width = query_weight.shape[1]
    cols = width // GROUPS

    def bit(d, c):
        return d if d > 1 else d ^ c

    def exchange(x, d):
        pairs = [(2 * i + c, 2 * (i ^ (1 << bit(d, c))) + c) for i in range(n) for c in range(2)]
        return lax.ppermute(x, ("gx", "yz"), pairs)

    bits = [(place >> j) & 1 for j in range(m)]
    where = [jnp.where(core == 0, bits[d], bits[bit(d, 1)]) for d in range(m)]

    def both(a, b, d, axis):
        first = where[d] == 0
        return jnp.stack([jnp.where(first, a, b), jnp.where(first, b, a)], axis)

    cube = [2] * m + [small]
    other = to_other_core(tokens)
    kv = jnp.dot(tokens, keyvalue_weight, preferred_element_type=F32).reshape(cube + [-1])

    def kv_chain(x):
        for d in range(m - 1):
            sent = pick(x, 1 - where[d], 0)
            x, got = yield pick(x, where[d], 0), sent, exchange(sent, d)
            x = x + got
        x, got = yield x, x, exchange(x, m - 1)
        x = (x + got).astype(BF16)
        for d in range(m - 2, -1, -1):
            x, got = yield x, x, exchange(x, d)
            x = both(x, got, d, 0)
        x = x.reshape(own, 2 * HEAD)
        x, got = yield x, x, to_other_core(x)
        return jnp.concatenate([x, got], 0)

    whole = jnp.stack([tokens, other]).reshape([2] + cube + [tokens.shape[1]])

    def product(rows, g, at):
        return jnp.dot(
            pick(rows, at, 1).reshape(total // 2, -1),
            query_weight[:, g * cols : (g + 1) * cols],
            preferred_element_type=F32,
        )

    def query_chain(g, rows):
        sent = half(product(rows, g, 1 - where[0]))
        x, got = yield None, sent, exchange(sent, 0)
        x = (x + full(got)).reshape([2] * m + [small, cols])
        for d in range(1, m):
            sent = half(pick(x, 1 - where[d], 1))
            x, got = yield pick(x, where[d], 1), sent, exchange(sent, d)
            x = x + full(got)
        return x.astype(BF16)

    def attention(query, keyvalue):
        positions = jnp.arange(own)
        key_pos = jnp.concatenate([positions + core * own, positions + (1 - core) * own])
        block = sum(where[d] << (m - 1 - d) for d in range(m))
        query_pos = block * small + jnp.arange(small)
        query_pos = jnp.concatenate([query_pos + core * own, query_pos + (1 - core) * own])
        allowed = (key_pos[None, :] <= query_pos[:, None]) & (
            key_pos[None, :] % PROMPTS == query_pos[:, None] % PROMPTS
        )
        grouped = query.reshape(span, -1, HEAD)
        scores = jnp.einsum("qhd,kd->hqk", grouped, keyvalue[:, :HEAD], preferred_element_type=F32)
        scores = jnp.where(allowed[None], scores * HEAD ** (-0.5), -1e30)
        probs = lax.optimization_barrier(jax.nn.softmax(scores, axis=-1).astype(BF16))
        out = jnp.einsum("hqk,kd->qhd", probs, keyvalue[:, HEAD:], preferred_element_type=F32)
        return out.astype(BF16).reshape(2, small, cols)

    def mixed_chain(x):
        for d in range(m - 1, -1, -1):
            x, got = yield x, x, exchange(x, d)
            x = both(x, got, d, 1)
        return x.reshape(total, cols)

    class Chain:
        def __init__(self, chain):
            self.chain, self.done = chain, None
            self.kept, self.sent, self.got = next(chain)

        def go(self, *made):
            kept, got = after((self.kept, self.got), *made)
            try:
                self.kept, self.sent, self.got = self.chain.send((kept, got))
            except StopIteration as stop:
                self.done = self.sent = stop.value

    class Sequence:
        def __init__(self):
            self.last = ()

        def go(self, chain, *made):
            chain.go(self.last, *made)
            self.last = chain.sent

        def open(self, chain):
            self.last = chain.sent
            return chain

        def rows(self):
            return after(whole, self.last)

    line = Sequence()
    k = line.open(Chain(kv_chain(kv)))
    q = [None] * GROUPS

    def send(g):
        q[g] = line.open(Chain(query_chain(g, line.rows())))

    def keep(g):
        q[g].kept = line.last = product(line.rows(), g, where[0])

    o = [None] * GROUPS

    def attend(g):
        line.go(q[g])
        o[g] = line.open(Chain(mixed_chain(attention(q[g].done, k.done))))

    def feed():
        if k.done is None:
            line.go(k)

    send(0)
    feed()
    for g in range(1, GROUPS):
        send(g)
        feed()
    for g in range(GROUPS):
        keep(g)
    waves = [(w, w - g, g) for w in range(1, m + GROUPS) for g in range(GROUPS - 1, -1, -1)]
    for w, s, g in waves:
        if 1 <= s < m:
            line.go(q[g])
            feed()
        elif s == m:
            while k.done is None:
                feed()
            attend(g)
    for s in range(1, m):
        for g in range(GROUPS):
            line.go(o[g])
    for g in range(GROUPS - 1):
        line.go(o[g])
    depth = (GROUPS - 1) * cols
    early = jnp.concatenate([x.done for x in o[:-1]], 1)
    early = jnp.dot(early, output_weight[:depth], preferred_element_type=F32)
    ours = early[:own] + to_other_core(early[own:])
    line.last = early
    line.go(o[-1])
    rest = o[-1].done
    theirs = jnp.dot(rest[own:], output_weight[depth:], preferred_element_type=F32).astype(BF16)
    came = to_other_core(theirs)
    rest = after(rest[:own], theirs)
    ours = ours + jnp.dot(rest, output_weight[depth:], preferred_element_type=F32)
    return (after(ours, came) + came.astype(F32)).astype(BF16)


def solution(mesh):
    return jax.shard_map(
        on_device,
        mesh=mesh,
        in_specs=(P(("groups", "yz"), "gx"), P("gx", "yz"), P("gx", None), P("yz", "gx")),
        out_specs=P(("groups", "yz"), "gx"),
        check_vma=False,
    )
```

time: 107 us -> 95.9 us (0.90)
  starting transfers between devices: 36.6 us -> 22.3 us
  waiting for transfers between devices: 33.2 us -> 42.3 us
  matrix products: 25.1 us -> 22 us
  other arithmetic: 6.13 us -> 4.56 us
    ppermute x29 -> x21, starting transfers between devices: 36.6 us -> 22.3 us  [the longest x17 19.8 us: exchange(): return lax.ppermute(x, ('gx', 'yz'), pairs)]
    ppermute x29 -> x21, waiting for transfers between devices: 33.2 us -> 42.3 us  [the longest x17 41.5 us: exchange(): return lax.ppermute(x, ('gx', 'yz'), pairs)]
    dot_general x11 -> x7, matrix products: 21.2 us -> 18.2 us  [the longest x4 9.31 us: product(): jnp.dot(pick(rows, at, 1).reshape(total // 2, -1), query_weight[:, g * co...]
    another operation x2 -> x1, other arithmetic: 2.77 us -> 1.33 us  [on_device(): whole = jnp.stack([tokens, other]).reshape([2] + cube + [tokens.shape[1]])]
  transfers between devices with their start and end apart: 29 -> 21, of which waited for: 15 -> 13; matrix products, arithmetic and copies ran while one was open for 29% -> 29% of each run, Pallas kernels for 0% -> 0%
where the time goes in v3:
time: 95.9 us; the launch traced here: 95.7 us
  waiting for transfers between devices  42.3 us (44%)
  starting transfers between devices  22.3 us (23%)
  matrix products  22 us (23%)
  other arithmetic  4.56 us (5%)
  local copies, waits for them, and re-layouts  3.92 us (4%)
    ppermute x17, waiting for transfers between devices, exchange(): return lax.ppermute(x, ('gx', 'yz'), pairs)  41.5 us
    ppermute x17, starting transfers between devices, exchange(): return lax.ppermute(x, ('gx', 'yz'), pairs)  19.8 us
    dot_general x4, matrix products, product(): jnp.dot(pick(rows, at, 1).reshape(total // 2, -1), query_weight[:, g * co...  9.31 us
    dot_general x1, matrix products, on_device(): early = jnp.dot(early, output_weight[:depth], preferred_element_type=F32)  5.76 us
    dot_general x1, matrix products, on_device(): jnp.dot(tokens, keyvalue_weight, preferred_element_type=F32)  2.54 us
    ppermute x4, starting transfers between devices, to_other_core(): return lax.ppermute(x, 'yz', [(0, 1), (1, 0)])  2.48 us
  transfers between devices with their start and end apart: 21, of which 13 were waited for; matrix products, arithmetic and copies ran while one was open for 29% of the time, Pallas kernels for 0%

profile of v3, /device:TPU:0, one launch (start us, length us, event | category | flops | bytes accessed | tf_op | source)
XLA Modules:
  0.0 95.7 jit_solution(7615821021778108869)
XLA Ops:
  0.0 0.5 collective-permute-start.1
  0.5 1.2 %copy-done = bf16[2304,512]{1,0:T(8,128)(2,1)S(1)} copy-done((bf16[2304,512]{1,0:T(8,128)(2,1)S(1)}, bf16[2304,512]{1,0:T(8,128)(2,1)}, u32[]{:S(2)}) %copy-start) | copy-done | bytes 2359320
  1.7 2.5 %fusion.73 = f32[192,512]{1,0:T(8,128)} fusion(bf16[192,2304]{1,0:T(8,128)(2,1)} %param.4, bf16[2304,512]{1,0:T(8,128)(2,1)S(1)} %copy-done), kind=kOutput, calls=%fused_computation.123 | convolution fusion | flops 452984832 | bytes 3637248 | tf_op jit(solution)/shard_map/dot_general | solution.py:63
  4.2 1.0 %dynamic-slice_bitcast_fusion.2 = (f32[2,2,24,512]{3,2,1,0:T(8,128)S(1)}, f32[2,2,24,512]{3,2,1,0:T(8,128)S(1)}) fusion(f32[2,2,2,24,512]{4,3,2,1,0:T(8,128)} %bitcast.140, s32[]{:T(128)S(6)} %select_n.156, s32[]{:T(128)S(6)} %select_n.155), kind=kLoop, calls=%fused_computation.79 | loop fusion | bytes 786440 | tf_op jit(solution)/shard_map/jit(dynamic_index_in_dim)/squeeze | solution.py:20
  5.3 3.0 %collective-permute-start = (f32[2,2,24,512]{3,2,1,0:T(8,128)S(1)}, f32[2,2,24,512]{3,2,1,0:T(8,128)S(1)}, u32[]{:S(2)}, u32[]{:S(2)}) collective-permute-start(f32[2,2,24,512]{3,2,1,0:T(8,128)S(1)} %get-tuple-element.107), channel_id=1, source_target_pairs={{0,2},{1,5},{2,0},{3,7},{4,6},{5,1},{6,4},{7,3},{8,10},{9,13},{10,... | collective-permute-start | bytes 589832 | tf_op jit(solution)/shard_map/ppermute | solution.py:52
  8.3 0.1 pad_add_fusion.1
  8.4 0.1 pad_add_fusion
  8.5 0.1 broadcast_compare_fusion
  8.6 1.3 %pad_maximum_fusion = bf16[2,2,2,2,24,2304]{5,4,3,2,1,0:T(8,128)(2,1)S(1)} fusion(bf16[1,2,2,2,24,2304]{5,4,3,2,1,0:T(8,128)(2,1)} %bitcast.4, bf16[1,2,2,2,24,2304]{5,4,3,2,1,0:T(8,128)(2,1)S(1)} %bitcast.131), kind=kLoop, calls=%fused_computation.23 | loop fusion | flops 884736 | bytes 3538944 | tf_op jit(solution)/shard_map/stack | solution.py:79
  10.0 4.7 %fusion.28 = f16[192,1536]{1,0:T(8,128)(2,1)S(1)} fusion(bf16[192,2304]{1,0:T(8,128)(2,1)S(1)} %bitcast.134, bf16[2304,3072]{1,0:T(8,128)(2,1)} %param.5), kind=kOutput, calls=%fused_computation.20 | convolution fusion | flops 1359544320 | bytes 8552448 | tf_op jit(solution)/shard_map/dot_general | solution.py:82
  14.8 1.6 %collective-permute-start.2 = (f32[2,24,512]{2,1,0:T(8,128)S(1)}, f32[2,24,512]{2,1,0:T(8,128)S(1)}, u32[]{:S(2)}, u32[]{:S(2)}) collective-permute-start(f32[2,24,512]{2,1,0:T(8,128)S(1)} %get-tuple-element.115), channel_id=1, source_target_pairs={{0,4},{1,3},{2,6},{3,1},{4,0},{5,7},{6,2},{7,5},{8,12},{9,11},{10,... | collective-permute-start | bytes 294920 | tf_op jit(solution)/shard_map/ppermute | solution.py:52
  16.4 0.5 collective-permute-start.4
  17.0 1.5 %fusion.25 = f16[192,1536]{1,0:T(8,128)(2,1)S(1)} fusion(bf16[192,2304]{1,0:T(8,128)(2,1)S(1)} %bitcast.133, bf16[2304,3072]{1,0:T(8,128)(2,1)S(1)} %copy-done.3), kind=kOutput, calls=%fused_computation.19 | convolution fusion | flops 1359544320 | bytes 8552448 | tf_op jit(solution)/shard_map/dot_general | solution.py:82
  18.6 1.6 %collective-permute-start.6 = (f16[192,1536]{1,0:T(8,128)(2,1)S(1)}, f16[192,1536]{1,0:T(8,128)(2,1)S(1)}, u32[]{:S(2)}, u32[]{:S(2)}) collective-permute-start(f16[192,1536]{1,0:T(8,128)(2,1)S(1)} %fusion.25), channel_id=1, source_target_pairs={{0,2},{1,5},{2,0},{3,7},{4,6},{5,1},{6,4},{7,3},{8,10},{9,13},{10,... | collective-permute-start | bytes 1769480 | tf_op jit(solution)/shard_map/ppermute | solution.py:52
  20.1 0.4 collective-permute-done.2
  20.5 2.7 %collective-permute-start.3 = (f32[2,24,512]{2,1,0:T(8,128)S(1)}, f32[2,24,512]{2,1,0:T(8,128)S(1)}, u32[]{:S(2)}, u32[]{:S(2)}) collective-permute-start(f32[2,24,512]{2,1,0:T(8,128)S(1)} %add.143), channel_id=1, source_target_pairs={{0,8},{1,9},{2,10},{3,11},{4,12},{5,13},{6,14},{7,15},{8,0},{9,1},... | collective-permute-start | bytes 294920 | tf_op jit(solution)/shard_map/ppermute | solution.py:52
  23.2 1.5 %fusion.12 = f32[192,1536]{1,0:T(8,128)S(1)} fusion(bf16[192,2304]{1,0:T(8,128)(2,1)S(1)} %bitcast.135, bf16[2304,3072]{1,0:T(8,128)(2,1)S(1)} %copy-done.3), kind=kOutput, calls=%fused_computation.12 | convolution fusion | flops 1358954496 | bytes 9142272 | tf_op jit(solution)/shard_map/dot_general | solution.py:82
  24.9 1.5 %fusion.8 = f32[192,1536]{1,0:T(8,128)S(1)} fusion(bf16[192,2304]{1,0:T(8,128)(2,1)S(1)} %bitcast.132, bf16[2304,3072]{1,0:T(8,128)(2,1)S(1)} %copy-done.3), kind=kOutput, calls=%fused_computation.8 | convolution fusion | flops 1358954496 | bytes 9142272 | tf_op jit(solution)/shard_map/dot_general | solution.py:82
  26.4 0.2 multiply_add_fusion.1
  26.6 0.1 constant_dynamic-slice_fusion.1
  26.8 1.7 %collective-permute-start.8 = (f16[2,2,24,1536]{3,2,0,1:T(8,128)(2,1)S(1)}, f16[2,2,24,1536]{3,2,0,1:T(8,128)(2,1)S(1)}, u32[]{:S(2)}, u32[]{:S(2)}) collective-permute-start(f16[2,2,24,1536]{3,2,0,1:T(8,128)(2,1)S(1)} %fusion.45), channel_id=1, source_target_pairs={{0,4},{1,3},{2,6},{3,1},{4,0},{5,7},{6,2},{7,5},{8,12},{9,11},{10,... | collective-permute-start | bytes 884744 | tf_op jit(solution)/shard_map/ppermute | solution.py:52
  28.5 0.5 collective-permute-start.5
  29.0 5.3 %collective-permute-done.6 = f16[192,1536]{1,0:T(8,128)(2,1)S(1)} collective-permute-done((f16[192,1536]{1,0:T(8,128)(2,1)S(1)}, f16[192,1536]{1,0:T(8,128)(2,1)S(1)}, u32[]{:S(2)}, u32[]{:S(2)}) %collective-permute-start.6) | collective-permute-done | bytes 589856 | tf_op jit(solution)/shard_map/ppermute | solution.py:52
  34.3 0.2 multiply_add_fusion
  34.5 0.1 constant_dynamic-slice_fusion
  34.7 1.4 %collective-permute-start.10 = (f16[2,2,24,1536]{3,2,0,1:T(8,128)(2,1)S(1)}, f16[2,2,24,1536]{3,2,0,1:T(8,128)(2,1)S(1)}, u32[]{:S(2)}, u32[]{:S(2)}) collective-permute-start(f16[2,2,24,1536]{3,2,0,1:T(8,128)(2,1)S(1)} %fusion.46), channel_id=1, source_target_pairs={{0,4},{1,3},{2,6},{3,1},{4,0},{5,7},{6,2},{7,5},{8,12},{9,11},{10,... | collective-permute-start | bytes 884744 | tf_op jit(solution)/shard_map/ppermute | solution.py:52
  36.1 1.6 %collective-permute-done.5 = bf16[2,24,512]{2,1,0:T(8,128)(2,1)S(1)} collective-permute-done((bf16[2,24,512]{2,1,0:T(8,128)(2,1)S(1)}, bf16[2,24,512]{2,1,0:T(8,128)(2,1)S(1)}, u32[]{:S(2)}, u32[]{:S(2)}) %collective-permute-start.5) | collective-permute-done | bytes 49184 | tf_op jit(solution)/shard_map/ppermute | solution.py:52
  37.8 0.2 collective-permute-start.7
  38.2 2.9 %collective-permute-start.11 = (f16[2,24,1536]{2,1,0:T(8,128)(2,1)S(1)}, f16[2,24,1536]{2,1,0:T(8,128)(2,1)S(1)}, u32[]{:S(2)}, u32[]{:S(2)}) collective-permute-start(f16[2,24,1536]{2,1,0:T(8,128)(2,1)S(1)} %get-tuple-element.104), channel_id=1, source_target_pairs={{0,8},{1,9},{2,10},{3,11},{4,12},{5,13},{6,14},{7,15},{8,0},{9,1},... | collective-permute-start | bytes 442376 | tf_op jit(solution)/shard_map/ppermute | solution.py:52
  41.1 2.3 %collective-permute-done.7 = bf16[2,2,24,512]{3,2,1,0:T(8,128)(2,1)S(1)} collective-permute-done((bf16[2,2,24,512]{3,2,1,0:T(8,128)(2,1)S(1)}, bf16[2,2,24,512]{3,2,1,0:T(8,128)(2,1)S(1)}, u32[]{:S(2)}, u32[]{:S(2)}) %collective-permute-start.7) | collective-permute-done | bytes 98336 | tf_op jit(solution)/shard_map/ppermute | solution.py:52
  43.5 1.8 %collective-permute-start.9 = (bf16[192,512]{1,0:T(8,128)(2,1)S(1)}, bf16[192,512]{1,0:T(8,128)(2,1)S(1)}, u32[]{:S(2)}, u32[]{:S(2)}) collective-permute-start(bf16[192,512]{1,0:T(8,128)(2,1)S(1)} %bitcast.136), channel_id=1, source_target_pairs={{0,1},{1,0},{2,3},{3,2},{4,5},{5,4},{6,7},{7,6},{8,9},{9,8},{10,11... | collective-permute-start | bytes 589832 | tf_op jit(solution)/shard_map/ppermute | solution.py:16
  45.4 1.5 %collective-permute-start.13 = (f16[2,24,1536]{2,1,0:T(8,128)(2,1)S(1)}, f16[2,24,1536]{2,1,0:T(8,128)(2,1)S(1)}, u32[]{:S(2)}, u32[]{:S(2)}) collective-permute-start(f16[2,24,1536]{2,1,0:T(8,128)(2,1)S(1)} %get-tuple-element.106), channel_id=1, source_target_pairs={{0,8},{1,9},{2,10},{3,11},{4,12},{5,13},{6,14},{7,15},{8,0},{9,1},... | collective-permute-start | bytes 442376 | tf_op jit(solution)/shard_map/ppermute | solution.py:52
  47.0 0.2 reshape.137
  47.2 0.4 fusion.67
  47.6 0.1 divide_convert_fusion.1
  47.8 0.2 fusion.40
  48.1 0.2 reshape.138
  48.2 1.5 %collective-permute-start.12 = (bf16[2,24,1536]{2,1,0:T(8,128)(2,1)S(1)}, bf16[2,24,1536]{2,1,0:T(8,128)(2,1)S(1)}, u32[]{:S(2)}, u32[]{:S(2)}) collective-permute-start(bf16[2,24,1536]{2,1,0:T(8,128)(2,1)S(1)} %reshape.138), channel_id=1, source_target_pairs={{0,8},{1,9},{2,10},{3,11},{4,12},{5,13},{6,14},{7,15},{8,0},{9,1},... | collective-permute-start | bytes 442376 | tf_op jit(solution)/shard_map/ppermute | solution.py:52
  49.8 9.7 %collective-permute-done.13 = f16[2,24,1536]{2,1,0:T(8,128)(2,1)S(1)} collective-permute-done((f16[2,24,1536]{2,1,0:T(8,128)(2,1)S(1)}, f16[2,24,1536]{2,1,0:T(8,128)(2,1)S(1)}, u32[]{:S(2)}, u32[]{:S(2)}) %collective-permute-start.13) | collective-permute-done | bytes 147488 | tf_op jit(solution)/shard_map/ppermute | solution.py:52
  59.5 0.2 reshape.139
  59.7 0.4 fusion.70
  60.2 0.1 divide_convert_fusion
  60.3 0.2 fusion.41
  60.6 0.2 reshape.140
  60.8 1.8 %collective-permute-done.12 = bf16[2,24,1536]{2,1,0:T(8,128)(2,1)S(1)} collective-permute-done((bf16[2,24,1536]{2,1,0:T(8,128)(2,1)S(1)}, bf16[2,24,1536]{2,1,0:T(8,128)(2,1)S(1)}, u32[]{:S(2)}, u32[]{:S(2)}) %collective-permute-start.12) | collective-permute-done | bytes 147488 | tf_op jit(solution)/shard_map/ppermute | solution.py:52
  62.7 0.3 collective-permute-start.14
  63.0 7.3 %collective-permute-done.15 = bf16[2,24,1536]{2,1,0:T(8,128)(2,1)S(1)} collective-permute-done((bf16[2,24,1536]{2,1,0:T(8,128)(2,1)S(1)}, bf16[2,24,1536]{2,1,0:T(8,128)(2,1)S(1)}, u32[]{:S(2)}, u32[]{:S(2)}) %collective-permute-start.15) | collective-permute-done | bytes 147488 | tf_op jit(solution)/shard_map/ppermute | solution.py:52
  70.4 2.1 %collective-permute-done.14 = bf16[2,2,24,1536]{3,2,0,1:T(8,128)(2,1)S(1)} collective-permute-done((bf16[2,2,24,1536]{3,2,0,1:T(8,128)(2,1)S(1)}, bf16[2,2,24,1536]{3,2,0,1:T(8,128)(2,1)S(1)}, u32[]{:S(2)}, u32[]{:S(2)}) %collective-permute-start.14) | collective-permute-done | bytes 294944 | tf_op jit(solution)/shard_map/ppermute | solution.py:52
  72.8 7.5 %collective-permute-done.17 = bf16[2,2,24,1536]{3,2,0,1:T(8,128)(2,1)S(1)} collective-permute-done((bf16[2,2,24,1536]{3,2,0,1:T(8,128)(2,1)S(1)}, bf16[2,2,24,1536]{3,2,0,1:T(8,128)(2,1)S(1)}, u32[]{:S(2)}, u32[]{:S(2)}) %collective-permute-start.17) | collective-permute-done | bytes 294944 | tf_op jit(solution)/shard_map/ppermute | solution.py:52
  80.4 2.2 %collective-permute-done.16 = bf16[2,2,2,24,1536]{4,3,0,2,1:T(8,128)(2,1)S(1)} collective-permute-done((bf16[2,2,2,24,1536]{4,3,0,2,1:T(8,128)(2,1)S(1)}, bf16[2,2,2,24,1536]{4,3,0,2,1:T(8,128)(2,1)S(1)}, u32[]{:S(2)}, u32[]{:S(2)}) %collective-permute-start.16) | collective-permute-done | bytes 589856 | tf_op jit(solution)/shard_map/ppermute | solution.py:52
  82.6 0.1 select_bitcast_fusion.3
  82.7 0.1 pad_maximum_fusion.1
  82.8 0.1 copy.24
  83.0 5.8 %fusion.2 = f32[384,2304]{1,0:T(8,128)S(1)} fusion(bf16[384,1536]{1,0:T(8,128)(2,1)S(1)} %bitcast.130, bf16[3072,2304]{1,0:T(8,128)(2,1)} %param.7), kind=kOutput, calls=%fused_computation.2 | convolution fusion | flops 2717908992 | bytes 11796480 | tf_op jit(solution)/shard_map/dot_general | solution.py:190
  88.7 0.1 slice.56
  88.9 0.2 collective-permute-start.18
  89.1 1.3 %collective-permute-done.19 = bf16[2,2,2,24,1536]{4,3,0,2,1:T(8,128)(2,1)S(1)} collective-permute-done((bf16[2,2,2,24,1536]{4,3,0,2,1:T(8,128)(2,1)S(1)}, bf16[2,2,2,24,1536]{4,3,0,2,1:T(8,128)(2,1)S(1)}, u32[]{:S(2)}, u32[]{:S(2)}) %collective-permute-start.19) | collective-permute-done | bytes 589856 | tf_op jit(solution)/shard_map/ppermute | solution.py:52
  90.3 0.1 select_bitcast_fusion
  90.5 0.1 pad_maximum_fusion.2
  90.6 1.5 %fusion.16 = bf16[192,2304]{1,0:T(8,128)(2,1)S(1)} fusion(bf16[192,1536]{1,0:T(8,128)(2,1)S(1)} %bitcast.139, bf16[3072,2304]{1,0:T(8,128)(2,1)S(1)} %bitcast.142), kind=kOutput, calls=%fused_computation.16 | convolution fusion | flops 1359396864 | bytes 8552448 | tf_op jit(solution)/shard_map/dot_general | solution.py:195
  92.2 0.4 collective-permute-done.18
  92.6 1.5 %fusion.31 = f32[192,2304]{1,0:T(8,128)S(1)} fusion(f32[192,2304]{1,0:T(8,128)S(1)} %collective-permute-done.18, f32[384,2304]{1,0:T(8,128)S(1)} %fusion.2, bf16[192,1536]{1,0:T(8,128)(2,1)S(1)} %bitcast.138, bf16[3072,2304]{1,0:T(8,128)(2,1)S(1)} %bitcast.142), kind=kOutput, calls=%fused_computation.22 | convolution fusion | flops 1359839232 | bytes 12976128 | tf_op jit(solution)/shard_map/dot_general | solution.py:198
  94.2 0.5 collective-permute-done.20
  94.7 1.1 %add_convert_fusion = bf16[192,2304]{1,0:T(8,128)(2,1)} fusion(f32[192,2304]{1,0:T(8,128)S(1)} %fusion.31, bf16[192,2304]{1,0:T(8,128)(2,1)S(1)} %collective-permute-done.20), kind=kLoop, calls=%fused_computation.24 | loop fusion | flops 1327104 | bytes 3538944 | tf_op jit(solution)/shard_map/convert_element_type | solution.py:199
  (65 shorter events, 1.8 us)
Async XLA Ops:
  0.0 1.7 %copy-start = (bf16[2304,512]{1,0:T(8,128)(2,1)S(1)}, bf16[2304,512]{1,0:T(8,128)(2,1)}, u32[]{:S(2)}) copy-start(bf16[2304,512]{1,0:T(8,128)(2,1)} %param.6) | copy-start | bytes 7077892
  0.0 8.6 %copy-start.2 = (bf16[192,2304]{1,0:T(8,128)(2,1)S(1)}, bf16[192,2304]{1,0:T(8,128)(2,1)}, u32[]{:S(2)}) copy-start(bf16[192,2304]{1,0:T(8,128)(2,1)} %param.4) | copy-start | bytes 2654212
  0.0 8.5 %collective-permute-start.1 = (bf16[192,2304]{1,0:T(8,128)(2,1)}, bf16[192,2304]{1,0:T(8,128)(2,1)}, u32[]{:S(2)}, u32[]{:S(2)}) collective-permute-start(bf16[192,2304]{1,0:T(8,128)(2,1)} %param.4), channel_id=1, source_target_pairs={{0,1},{1,0},{2,3},{3,2},{4,5},{5,4},{6,7},{7,6},{8,9},{9,8},{10,11... | collective-permute-start | bytes 2654216 | tf_op jit(solution)/shard_map/ppermute | solution.py:16
  5.3 9.4 %collective-permute-start = (f32[2,2,24,512]{3,2,1,0:T(8,128)S(1)}, f32[2,2,24,512]{3,2,1,0:T(8,128)S(1)}, u32[]{:S(2)}, u32[]{:S(2)}) collective-permute-start(f32[2,2,24,512]{3,2,1,0:T(8,128)S(1)} %get-tuple-element.107), channel_id=1, source_target_pairs={{0,2},{1,5},{2,0},{3,7},{4,6},{5,1},{6,4},{7,3},{8,10},{9,13},{10,... | collective-permute-start | bytes 589832 | tf_op jit(solution)/shard_map/ppermute | solution.py:52
  10.0 7.0 %copy-start.3 = (bf16[2304,3072]{1,0:T(8,128)(2,1)S(1)}, bf16[2304,3072]{1,0:T(8,128)(2,1)}, u32[]{:S(2)}) copy-start(bf16[2304,3072]{1,0:T(8,128)(2,1)} %param.5) | copy-start | bytes 42467332
  14.8 5.7 %collective-permute-start.2 = (f32[2,24,512]{2,1,0:T(8,128)S(1)}, f32[2,24,512]{2,1,0:T(8,128)S(1)}, u32[]{:S(2)}, u32[]{:S(2)}) collective-permute-start(f32[2,24,512]{2,1,0:T(8,128)S(1)} %get-tuple-element.115), channel_id=1, source_target_pairs={{0,4},{1,3},{2,6},{3,1},{4,0},{5,7},{6,2},{7,5},{8,12},{9,11},{10,... | collective-permute-start | bytes 294920 | tf_op jit(solution)/shard_map/ppermute | solution.py:52
  16.4 10.0 %collective-permute-start.4 = (f16[192,1536]{1,0:T(8,128)(2,1)S(1)}, f16[192,1536]{1,0:T(8,128)(2,1)S(1)}, u32[]{:S(2)}, u32[]{:S(2)}) collective-permute-start(f16[192,1536]{1,0:T(8,128)(2,1)S(1)} %fusion.28), channel_id=1, source_target_pairs={{0,2},{1,5},{2,0},{3,7},{4,6},{5,1},{6,4},{7,3},{8,10},{9,13},{10,... | collective-permute-start | bytes 1769480 | tf_op jit(solution)/shard_map/ppermute | solution.py:52
  18.6 15.7 %collective-permute-start.6 = (f16[192,1536]{1,0:T(8,128)(2,1)S(1)}, f16[192,1536]{1,0:T(8,128)(2,1)S(1)}, u32[]{:S(2)}, u32[]{:S(2)}) collective-permute-start(f16[192,1536]{1,0:T(8,128)(2,1)S(1)} %fusion.25), channel_id=1, source_target_pairs={{0,2},{1,5},{2,0},{3,7},{4,6},{5,1},{6,4},{7,3},{8,10},{9,13},{10,... | collective-permute-start | bytes 1769480 | tf_op jit(solution)/shard_map/ppermute | solution.py:52
  20.5 7.9 %collective-permute-start.3 = (f32[2,24,512]{2,1,0:T(8,128)S(1)}, f32[2,24,512]{2,1,0:T(8,128)S(1)}, u32[]{:S(2)}, u32[]{:S(2)}) collective-permute-start(f32[2,24,512]{2,1,0:T(8,128)S(1)} %add.143), channel_id=1, source_target_pairs={{0,8},{1,9},{2,10},{3,11},{4,12},{5,13},{6,14},{7,15},{8,0},{9,1},... | collective-permute-start | bytes 294920 | tf_op jit(solution)/shard_map/ppermute | solution.py:52
  26.8 11.3 %collective-permute-start.8 = (f16[2,2,24,1536]{3,2,0,1:T(8,128)(2,1)S(1)}, f16[2,2,24,1536]{3,2,0,1:T(8,128)(2,1)S(1)}, u32[]{:S(2)}, u32[]{:S(2)}) collective-permute-start(f16[2,2,24,1536]{3,2,0,1:T(8,128)(2,1)S(1)} %fusion.45), channel_id=1, source_target_pairs={{0,4},{1,3},{2,6},{3,1},{4,0},{5,7},{6,2},{7,5},{8,12},{9,11},{10,... | collective-permute-start | bytes 884744 | tf_op jit(solution)/shard_map/ppermute | solution.py:52
  28.5 9.3 %collective-permute-start.5 = (bf16[2,24,512]{2,1,0:T(8,128)(2,1)S(1)}, bf16[2,24,512]{2,1,0:T(8,128)(2,1)S(1)}, u32[]{:S(2)}, u32[]{:S(2)}) collective-permute-start(bf16[2,24,512]{2,1,0:T(8,128)(2,1)S(1)} %add_convert_fusion.3), channel_id=1, source_target_pairs={{0,4},{1,3},{2,6},{3,1},{4,0},{5,7},{6,2},{7,5},{8,12},{9,11},{10,... | collective-permute-start | bytes 147464 | tf_op jit(solution)/shard_map/ppermute | solution.py:52
  34.7 10.5 %collective-permute-start.10 = (f16[2,2,24,1536]{3,2,0,1:T(8,128)(2,1)S(1)}, f16[2,2,24,1536]{3,2,0,1:T(8,128)(2,1)S(1)}, u32[]{:S(2)}, u32[]{:S(2)}) collective-permute-start(f16[2,2,24,1536]{3,2,0,1:T(8,128)(2,1)S(1)} %fusion.46), channel_id=1, source_target_pairs={{0,4},{1,3},{2,6},{3,1},{4,0},{5,7},{6,2},{7,5},{8,12},{9,11},{10,... | collective-permute-start | bytes 884744 | tf_op jit(solution)/shard_map/ppermute | solution.py:52
  37.8 5.7 %collective-permute-start.7 = (bf16[2,2,24,512]{3,2,1,0:T(8,128)(2,1)S(1)}, bf16[2,2,24,512]{3,2,1,0:T(8,128)(2,1)S(1)}, u32[]{:S(2)}, u32[]{:S(2)}) collective-permute-start(bf16[2,2,24,512]{3,2,1,0:T(8,128)(2,1)S(1)} %pad_maximum_fusion.8), channel_id=1, source_target_pairs={{0,2},{1,5},{2,0},{3,7},{4,6},{5,1},{6,4},{7,3},{8,10},{9,13},{10,... | collective-permute-start | bytes 294920 | tf_op jit(solution)/shard_map/ppermute | solution.py:52
  38.2 8.8 %collective-permute-start.11 = (f16[2,24,1536]{2,1,0:T(8,128)(2,1)S(1)}, f16[2,24,1536]{2,1,0:T(8,128)(2,1)S(1)}, u32[]{:S(2)}, u32[]{:S(2)}) collective-permute-start(f16[2,24,1536]{2,1,0:T(8,128)(2,1)S(1)} %get-tuple-element.104), channel_id=1, source_target_pairs={{0,8},{1,9},{2,10},{3,11},{4,12},{5,13},{6,14},{7,15},{8,0},{9,1},... | collective-permute-start | bytes 442376 | tf_op jit(solution)/shard_map/ppermute | solution.py:52
  43.5 3.4 %collective-permute-start.9 = (bf16[192,512]{1,0:T(8,128)(2,1)S(1)}, bf16[192,512]{1,0:T(8,128)(2,1)S(1)}, u32[]{:S(2)}, u32[]{:S(2)}) collective-permute-start(bf16[192,512]{1,0:T(8,128)(2,1)S(1)} %bitcast.136), channel_id=1, source_target_pairs={{0,1},{1,0},{2,3},{3,2},{4,5},{5,4},{6,7},{7,6},{8,9},{9,8},{10,11... | collective-permute-start | bytes 589832 | tf_op jit(solution)/shard_map/ppermute | solution.py:16
  45.4 14.1 %collective-permute-start.13 = (f16[2,24,1536]{2,1,0:T(8,128)(2,1)S(1)}, f16[2,24,1536]{2,1,0:T(8,128)(2,1)S(1)}, u32[]{:S(2)}, u32[]{:S(2)}) collective-permute-start(f16[2,24,1536]{2,1,0:T(8,128)(2,1)S(1)} %get-tuple-element.106), channel_id=1, source_target_pairs={{0,8},{1,9},{2,10},{3,11},{4,12},{5,13},{6,14},{7,15},{8,0},{9,1},... | collective-permute-start | bytes 442376 | tf_op jit(solution)/shard_map/ppermute | solution.py:52
  48.2 14.4 %collective-permute-start.12 = (bf16[2,24,1536]{2,1,0:T(8,128)(2,1)S(1)}, bf16[2,24,1536]{2,1,0:T(8,128)(2,1)S(1)}, u32[]{:S(2)}, u32[]{:S(2)}) collective-permute-start(bf16[2,24,1536]{2,1,0:T(8,128)(2,1)S(1)} %reshape.138), channel_id=1, source_target_pairs={{0,8},{1,9},{2,10},{3,11},{4,12},{5,13},{6,14},{7,15},{8,0},{9,1},... | collective-permute-start | bytes 442376 | tf_op jit(solution)/shard_map/ppermute | solution.py:52
  60.8 9.5 %collective-permute-start.15 = (bf16[2,24,1536]{2,1,0:T(8,128)(2,1)S(1)}, bf16[2,24,1536]{2,1,0:T(8,128)(2,1)S(1)}, u32[]{:S(2)}, u32[]{:S(2)}) collective-permute-start(bf16[2,24,1536]{2,1,0:T(8,128)(2,1)S(1)} %reshape.140), channel_id=1, source_target_pairs={{0,8},{1,9},{2,10},{3,11},{4,12},{5,13},{6,14},{7,15},{8,0},{9,1},... | collective-permute-start | bytes 442376 | tf_op jit(solution)/shard_map/ppermute | solution.py:52
  62.7 9.8 %collective-permute-start.14 = (bf16[2,2,24,1536]{3,2,0,1:T(8,128)(2,1)S(1)}, bf16[2,2,24,1536]{3,2,0,1:T(8,128)(2,1)S(1)}, u32[]{:S(2)}, u32[]{:S(2)}) collective-permute-start(bf16[2,2,24,1536]{3,2,0,1:T(8,128)(2,1)S(1)} %pad_maximum_fusion.5), channel_id=1, source_target_pairs={{0,4},{1,3},{2,6},{3,1},{4,0},{5,7},{6,2},{7,5},{8,12},{9,11},{10,... | collective-permute-start | bytes 884744 | tf_op jit(solution)/shard_map/ppermute | solution.py:52
  70.3 9.9 %collective-permute-start.17 = (bf16[2,2,24,1536]{3,2,0,1:T(8,128)(2,1)S(1)}, bf16[2,2,24,1536]{3,2,0,1:T(8,128)(2,1)S(1)}, u32[]{:S(2)}, u32[]{:S(2)}) collective-permute-start(bf16[2,2,24,1536]{3,2,0,1:T(8,128)(2,1)S(1)} %pad_maximum_fusion.6), channel_id=1, source_target_pairs={{0,4},{1,3},{2,6},{3,1},{4,0},{5,7},{6,2},{7,5},{8,12},{9,11},{10,... | collective-permute-start | bytes 884744 | tf_op jit(solution)/shard_map/ppermute | solution.py:52
  72.7 9.9 %collective-permute-start.16 = (bf16[2,2,2,24,1536]{4,3,0,2,1:T(8,128)(2,1)S(1)}, bf16[2,2,2,24,1536]{4,3,0,2,1:T(8,128)(2,1)S(1)}, u32[]{:S(2)}, u32[]{:S(2)}) collective-permute-start(bf16[2,2,2,24,1536]{4,3,0,2,1:T(8,128)(2,1)S(1)} %pad_maximum_fusion.3), channel_id=1, source_target_pairs={{0,2},{1,5},{2,0},{3,7},{4,6},{5,1},{6,4},{7,3},{8,10},{9,13},{10,... | collective-permute-start | bytes 1769480 | tf_op jit(solution)/shard_map/ppermute | solution.py:52
  80.4 9.9 %collective-permute-start.19 = (bf16[2,2,2,24,1536]{4,3,0,2,1:T(8,128)(2,1)S(1)}, bf16[2,2,2,24,1536]{4,3,0,2,1:T(8,128)(2,1)S(1)}, u32[]{:S(2)}, u32[]{:S(2)}) collective-permute-start(bf16[2,2,2,24,1536]{4,3,0,2,1:T(8,128)(2,1)S(1)} %pad_maximum_fusion.4), channel_id=1, source_target_pairs={{0,2},{1,5},{2,0},{3,7},{4,6},{5,1},{6,4},{7,3},{8,10},{9,13},{10,... | collective-permute-start | bytes 1769480 | tf_op jit(solution)/shard_map/ppermute | solution.py:52
  82.8 7.7 %slice-start = ((s8[14155776]{0:T(1024)(128)(4,1)}), s8[4194304]{0:T(1024)(128)(4,1)S(1)}, s32[]{:S(2)}) async-start(s8[14155776]{0:T(1024)(128)(4,1)} %bitcast.141), calls=%async_computation | async-start | bytes 8388608
  83.0 7.6 %slice-start.1 = ((s8[14155776]{0:T(1024)(128)(4,1)}), s8[4194304]{0:T(1024)(128)(4,1)S(1)}, s32[]{:S(2)}) async-start(s8[14155776]{0:T(1024)(128)(4,1)} %bitcast.141), calls=%async_computation.1 | async-start | bytes 8388608
  83.0 7.6 %slice-start.2 = ((s8[14155776]{0:T(1024)(128)(4,1)}), s8[4194304]{0:T(1024)(128)(4,1)S(1)}, s32[]{:S(2)}) async-start(s8[14155776]{0:T(1024)(128)(4,1)} %bitcast.141), calls=%async_computation.2 | async-start | bytes 8388608
  83.0 7.6 %slice-start.3 = ((s8[14155776]{0:T(1024)(128)(4,1)}), s8[1572864]{0:T(1024)(128)(4,1)S(1)}, s32[]{:S(2)}) async-start(s8[14155776]{0:T(1024)(128)(4,1)} %bitcast.141), calls=%async_computation.3 | async-start | bytes 3145728
  88.9 3.8 %collective-permute-start.18 = (f32[192,2304]{1,0:T(8,128)S(1)}, f32[192,2304]{1,0:T(8,128)S(1)}, u32[]{:S(2)}, u32[]{:S(2)}) collective-permute-start(f32[192,2304]{1,0:T(8,128)S(1)} %slice.56), channel_id=1, source_target_pairs={{0,1},{1,0},{2,3},{3,2},{4,5},{5,4},{6,7},{7,6},{8,9},{9,8},{10,11... | collective-permute-start | bytes 5308424 | tf_op jit(solution)/shard_map/ppermute | solution.py:16
  92.2 2.5 %collective-permute-start.20 = (bf16[192,2304]{1,0:T(8,128)(2,1)S(1)}, bf16[192,2304]{1,0:T(8,128)(2,1)S(1)}, u32[]{:S(2)}, u32[]{:S(2)}) collective-permute-start(bf16[192,2304]{1,0:T(8,128)(2,1)S(1)} %fusion.16), channel_id=1, source_target_pairs={{0,1},{1,0},{2,3},{3,2},{4,5},{5,4},{6,7},{7,6},{8,9},{9,8},{10,11... | collective-permute-start | bytes 2654216 | tf_op jit(solution)/shard_map/ppermute | solution.py:16
  92.6 3.1 %copy-start.1 = (bf16[2304,512]{1,0:T(8,128)(2,1)S(1)}, bf16[2304,512]{1,0:T(8,128)(2,1)}, u32[]{:S(2)}) copy-start(bf16[2304,512]{1,0:T(8,128)(2,1)} %param.6) | copy-start | bytes 7077892

commit v4 on v3

--- a/solution.py
+++ b/solution.py
@@ -1,6 +1,8 @@
 import jax
 import jax.numpy as jnp
 from jax import lax
+from jax.experimental import pallas as pl
+from jax.experimental.pallas import tpu as pltpu
 from jax.sharding import PartitionSpec as P
 
 HEAD = 256
@@ -26,6 +28,46 @@
 
 def full(x):
     return x.astype(F32) * (1.0 / SCALE)
+
+
+def halves_kernel(at, x, w, sent, kept, rows, near, sem):
+    size = sent.shape[0]
+    copies = [
+        pltpu.make_async_copy(
+            x.at[pl.ds(pl.multiple_of(half_of * size, size), size)],
+            rows.at[pl.ds(i * size, size)],
+            sem.at[i],
+        )
+        for i, half_of in enumerate((1 - at[0], at[0]))
+    ]
+    copies.append(pltpu.make_async_copy(w, near, sem.at[2]))
+    for copy in copies:
+        copy.start()
+    for copy in copies:
+        copy.wait()
+    out = jnp.dot(rows[...], near[...], preferred_element_type=F32)
+    sent[...] = out[:size]
+    kept[...] = out[size:]
+
+
+def halves(x, w, at):
+    out = jax.ShapeDtypeStruct((x.shape[0] // 2, w.shape[1]), F32)
+    anywhere, vmem = pl.BlockSpec(memory_space=pl.ANY), pl.BlockSpec(memory_space=pltpu.VMEM)
+    return pl.pallas_call(
+        halves_kernel,
+        out_shape=[out, out],
+        in_specs=[pl.BlockSpec(memory_space=pltpu.SMEM), anywhere, anywhere],
+        out_specs=[vmem, vmem],
+        scratch_shapes=[
+            pltpu.VMEM(x.shape, x.dtype),
+            pltpu.VMEM(w.shape, w.dtype),
+            pltpu.SemaphoreType.DMA((3,)),
+        ],
+        compiler_params=pltpu.CompilerParams(vmem_limit_bytes=56 << 20),
+        cost_estimate=pl.CostEstimate(
+            flops=2 * x.size * w.shape[1], bytes_accessed=2 * (x.size + w.size), transcendentals=0
+        ),
+    )(at.astype(jnp.int32).reshape(1), x, w)
 
 
 def after(x, *made):
@@ -60,10 +102,12 @@
 
     cube = [2] * m + [small]
     other = to_other_core(tokens)
-    kv = jnp.dot(tokens, keyvalue_weight, preferred_element_type=F32).reshape(cube + [-1])
-
-    def kv_chain(x):
-        for d in range(m - 1):
+
+    def kv_chain():
+        sent, x = halves(tokens, keyvalue_weight, where[0])
+        x, got = yield x, sent, exchange(sent, 0)
+        x = (x + got).reshape(cube[1:] + [2 * HEAD])
+        for d in range(1, m - 1):
             sent = pick(x, 1 - where[d], 0)
             x, got = yield pick(x, where[d], 0), sent, exchange(sent, d)
             x = x + got
@@ -145,7 +189,7 @@
             return after(whole, self.last)
 
     line = Sequence()
-    k = line.open(Chain(kv_chain(kv)))
+    k = line.open(Chain(kv_chain()))
     q = [None] * GROUPS
 
     def send(g):
@@ -164,22 +208,18 @@
         if k.done is None:
             line.go(k)
 
-    send(0)
-    feed()
-    for g in range(1, GROUPS):
+    for g in range(GROUPS):
         send(g)
         feed()
-    for g in range(GROUPS):
         keep(g)
-    waves = [(w, w - g, g) for w in range(1, m + GROUPS) for g in range(GROUPS - 1, -1, -1)]
-    for w, s, g in waves:
-        if 1 <= s < m:
+    for s in range(1, m):
+        for g in range(GROUPS):
             line.go(q[g])
             feed()
-        elif s == m:
-            while k.done is None:
-                feed()
-            attend(g)
+    while k.done is None:
+        feed()
+    for g in range(GROUPS):
+        attend(g)
     for s in range(1, m):
         for g in range(GROUPS):
             line.go(o[g])
@@ -188,14 +228,14 @@
     depth = (GROUPS - 1) * cols
     early = jnp.concatenate([x.done for x in o[:-1]], 1)
     early = jnp.dot(early, output_weight[:depth], preferred_element_type=F32)
-    ours = early[:own] + to_other_core(early[own:])
     line.last = early
     line.go(o[-1])
     rest = o[-1].done
-    theirs = jnp.dot(rest[own:], output_weight[depth:], preferred_element_type=F32).astype(BF16)
+    theirs = jnp.dot(rest[own:], output_weight[depth:], preferred_element_type=F32)
+    theirs = (early[own:] + theirs).astype(BF16)
     came = to_other_core(theirs)
     rest = after(rest[:own], theirs)
-    ours = ours + jnp.dot(rest, output_weight[depth:], preferred_element_type=F32)
+    ours = early[:own] + jnp.dot(rest, output_weight[depth:], preferred_element_type=F32)
     return (after(ours, came) + came.astype(F32)).astype(BF16)
 
 

time: 95.9 us -> 92 us (0.959)
  waiting for transfers between devices: 42.3 us -> 36.2 us
  starting transfers between devices: 22.3 us -> 27.3 us
  Pallas kernels: 0 us -> 3.3 us
  matrix products: 22 us -> 19.6 us
  local copies, waits for them, and re-layouts: 3.92 us -> 1.57 us
  other arithmetic: 4.56 us -> 3.3 us
    ppermute x17, waiting for transfers between devices: 41.5 us -> 35.3 us  [exchange(): return lax.ppermute(x, ('gx', 'yz'), pairs)]
    ppermute x17, starting transfers between devices: 19.8 us -> 24.5 us  [exchange(): return lax.ppermute(x, ('gx', 'yz'), pairs)]
    pallas_call x0 -> x1, Pallas kernels: none -> 3.3 us  [halves(): pl.pallas_call(halves_kernel, out_shape=[out, out], in_specs=[pl.BlockSpe...]
    dot_general x1 -> x0, matrix products: 2.54 us -> none  [on_device(): jnp.dot(tokens, keyvalue_weight, preferred_element_type=F32)]
    unnamed x17 -> x15, local copies, waits for them, and re-layouts: 1.29 us -> 0.08 us
    another operation x1, other arithmetic: 1.33 us -> 0.16 us  [on_device(): whole = jnp.stack([tokens, other]).reshape([2] + cube + [tokens.shape[1]])]
    squeeze x2 -> x1, local copies, waits for them, and re-layouts: 1.07 us -> 0.02 us  [pick(): return lax.dynamic_index_in_dim(x, at, axis, keepdims=False)]
    ppermute x4 -> x3, starting transfers between devices: 2.48 us -> 2.8 us  [to_other_core(): return lax.ppermute(x, 'yz', [(0, 1), (1, 0)])]
  transfers between devices with their start and end apart: 21 -> 20, of which waited for: 13 -> 13; matrix products, arithmetic and copies ran while one was open for 29% -> 23% of each run, Pallas kernels for 0% -> 4%
where the time goes in v4:
time: 92 us; the launch traced here: 91.8 us
  waiting for transfers between devices  36.2 us (39%)
  starting transfers between devices  27.3 us (30%)
  matrix products  19.6 us (21%)
  Pallas kernels  3.3 us (4%)
  other arithmetic  3.3 us (4%)
  local copies, waits for them, and re-layouts  1.57 us (2%)
    ppermute x17, waiting for transfers between devices, exchange(): return lax.ppermute(x, ('gx', 'yz'), pairs)  35.3 us
    ppermute x17, starting transfers between devices, exchange(): return lax.ppermute(x, ('gx', 'yz'), pairs)  24.5 us
    dot_general x4, matrix products, product(): jnp.dot(pick(rows, at, 1).reshape(total // 2, -1), query_weight[:, g * co...  9.31 us
    dot_general x1, matrix products, on_device(): early = jnp.dot(early, output_weight[:depth], preferred_element_type=F32)  5.86 us
    pallas_call x1, Pallas kernels, halves(): pl.pallas_call(halves_kernel, out_shape=[out, out], in_specs=[pl.BlockSpe...  3.3 us
    ppermute x3, starting transfers between devices, to_other_core(): return lax.ppermute(x, 'yz', [(0, 1), (1, 0)])  2.8 us
  transfers between devices with their start and end apart: 20, of which 13 were waited for; matrix products, arithmetic and copies ran while one was open for 23% of the time, Pallas kernels for 4%

profile of v4, /device:TPU:0, one launch (start us, length us, event | category | flops | bytes accessed | tf_op | source)
XLA Modules:
  0.0 91.8 jit_solution(3593123254094982671)
XLA Ops:
  0.0 0.5 collective-permute-start.1
  0.5 3.3 %shard_map.46 = (f32[96,512]{1,0:T(8,128)}, f32[96,512]{1,0:T(8,128)}) custom-call(s32[1]{0:T(128)} %bitcast.at, bf16[192,2304]{1,0:T(8,128)(2,1)} %x.1, bf16[2304,512]{1,0:T(8,128)(2,1)} %w.1), custom_call_target="tpu_custom_call" | custom-call | flops 452984832 | bytes 3244032 | tf_op jit(solution)/shard_map/pallas_call | solution.py:56
  3.8 2.6 %collective-permute-start = (f32[96,512]{1,0:T(8,128)}, f32[96,512]{1,0:T(8,128)S(1)}, u32[]{:S(2)}, u32[]{:S(2)}) collective-permute-start(f32[96,512]{1,0:T(8,128)} %get-tuple-element.50), channel_id=1, source_target_pairs={{0,2},{1,5},{2,0},{3,7},{4,6},{5,1},{6,4},{7,3},{8,10},{9,13},{10,... | collective-permute-start | bytes 589832 | tf_op jit(solution)/shard_map/ppermute | solution.py:94
  6.4 0.1 pad_add_fusion.1
  6.5 0.1 pad_add_fusion
  6.6 0.1 broadcast_compare_fusion
  6.7 0.2 pad_maximum_fusion
  7.0 4.7 %fusion.34 = f16[192,1536]{1,0:T(8,128)(2,1)S(1)} fusion(bf16[192,2304]{1,0:T(8,128)(2,1)S(1)} %bitcast.130, bf16[2304,3072]{1,0:T(8,128)(2,1)} %param.5), kind=kOutput, calls=%fused_computation.22 | convolution fusion | flops 1359544320 | bytes 8552448 | tf_op jit(solution)/shard_map/dot_general | solution.py:126
  11.7 1.6 %collective-permute-start.2 = (f32[2,24,512]{2,1,0:T(8,128)S(1)}, f32[2,24,512]{2,1,0:T(8,128)S(1)}, u32[]{:S(2)}, u32[]{:S(2)}) collective-permute-start(f32[2,24,512]{2,1,0:T(8,128)S(1)} %get-tuple-element.117), channel_id=1, source_target_pairs={{0,4},{1,3},{2,6},{3,1},{4,0},{5,7},{6,2},{7,5},{8,12},{9,11},{10,... | collective-permute-start | bytes 294920 | tf_op jit(solution)/shard_map/ppermute | solution.py:94
  13.4 0.6 collective-permute-start.4
  14.1 1.5 %fusion.12 = f32[192,1536]{1,0:T(8,128)S(1)} fusion(bf16[192,2304]{1,0:T(8,128)(2,1)S(1)} %bitcast.131, bf16[2304,3072]{1,0:T(8,128)(2,1)S(1)} %copy-done.2), kind=kOutput, calls=%fused_computation.12 | convolution fusion | flops 1358954496 | bytes 9142272 | tf_op jit(solution)/shard_map/dot_general | solution.py:126
  15.7 1.5 %fusion.31 = f16[192,1536]{1,0:T(8,128)(2,1)S(1)} fusion(bf16[192,2304]{1,0:T(8,128)(2,1)S(1)} %bitcast.129, bf16[2304,3072]{1,0:T(8,128)(2,1)S(1)} %copy-done.2), kind=kOutput, calls=%fused_computation.21 | convolution fusion | flops 1359544320 | bytes 8552448 | tf_op jit(solution)/shard_map/dot_general | solution.py:126
  17.3 1.5 %collective-permute-start.6 = (f16[192,1536]{1,0:T(8,128)(2,1)S(1)}, f16[192,1536]{1,0:T(8,128)(2,1)S(1)}, u32[]{:S(2)}, u32[]{:S(2)}) collective-permute-start(f16[192,1536]{1,0:T(8,128)(2,1)S(1)} %fusion.31), channel_id=1, source_target_pairs={{0,2},{1,5},{2,0},{3,7},{4,6},{5,1},{6,4},{7,3},{8,10},{9,13},{10,... | collective-permute-start | bytes 1769480 | tf_op jit(solution)/shard_map/ppermute | solution.py:94
  18.7 2.7 %collective-permute-start.3 = (f32[2,24,512]{2,1,0:T(8,128)S(1)}, f32[2,24,512]{2,1,0:T(8,128)S(1)}, u32[]{:S(2)}, u32[]{:S(2)}) collective-permute-start(f32[2,24,512]{2,1,0:T(8,128)S(1)} %add.140), channel_id=1, source_target_pairs={{0,8},{1,9},{2,10},{3,11},{4,12},{5,13},{6,14},{7,15},{8,0},{9,1},... | collective-permute-start | bytes 294920 | tf_op jit(solution)/shard_map/ppermute | solution.py:94
  21.5 1.5 %fusion.8 = f32[192,1536]{1,0:T(8,128)S(1)} fusion(bf16[192,2304]{1,0:T(8,128)(2,1)S(1)} %bitcast.128, bf16[2304,3072]{1,0:T(8,128)(2,1)S(1)} %copy-done.2), kind=kOutput, calls=%fused_computation.8 | convolution fusion | flops 1358954496 | bytes 9142272 | tf_op jit(solution)/shard_map/dot_general | solution.py:126
  23.0 0.3 collective-permute-done.4
  23.3 0.2 multiply_add_fusion.1
  23.4 0.1 constant_dynamic-slice_fusion.1
  23.6 0.5 collective-permute-start.8
  24.1 1.1 %collective-permute-done.3 = f32[2,24,512]{2,1,0:T(8,128)S(1)} collective-permute-done((f32[2,24,512]{2,1,0:T(8,128)S(1)}, f32[2,24,512]{2,1,0:T(8,128)S(1)}, u32[]{:S(2)}, u32[]{:S(2)}) %collective-permute-start.3) | collective-permute-done | bytes 98336 | tf_op jit(solution)/shard_map/ppermute | solution.py:94
  25.2 1.0 %collective-permute-start.5 = (bf16[2,24,512]{2,1,0:T(8,128)(2,1)S(1)}, bf16[2,24,512]{2,1,0:T(8,128)(2,1)S(1)}, u32[]{:S(2)}, u32[]{:S(2)}) collective-permute-start(bf16[2,24,512]{2,1,0:T(8,128)(2,1)S(1)} %add_convert_fusion.3), channel_id=1, source_target_pairs={{0,4},{1,3},{2,6},{3,1},{4,0},{5,7},{6,2},{7,5},{8,12},{9,11},{10,... | collective-permute-start | bytes 147464 | tf_op jit(solution)/shard_map/ppermute | solution.py:94
  26.2 5.3 %collective-permute-done.6 = f16[192,1536]{1,0:T(8,128)(2,1)S(1)} collective-permute-done((f16[192,1536]{1,0:T(8,128)(2,1)S(1)}, f16[192,1536]{1,0:T(8,128)(2,1)S(1)}, u32[]{:S(2)}, u32[]{:S(2)}) %collective-permute-start.6) | collective-permute-done | bytes 589856 | tf_op jit(solution)/shard_map/ppermute | solution.py:94
  31.5 0.2 multiply_add_fusion
  31.7 0.1 constant_dynamic-slice_fusion
  31.9 1.6 %collective-permute-start.10 = (f16[2,2,24,1536]{3,2,0,1:T(8,128)(2,1)S(1)}, f16[2,2,24,1536]{3,2,0,1:T(8,128)(2,1)S(1)}, u32[]{:S(2)}, u32[]{:S(2)}) collective-permute-start(f16[2,2,24,1536]{3,2,0,1:T(8,128)(2,1)S(1)} %fusion.51), channel_id=1, source_target_pairs={{0,4},{1,3},{2,6},{3,1},{4,0},{5,7},{6,2},{7,5},{8,12},{9,11},{10,... | collective-permute-start | bytes 884744 | tf_op jit(solution)/shard_map/ppermute | solution.py:94
  33.5 1.2 %collective-permute-done.5 = bf16[2,24,512]{2,1,0:T(8,128)(2,1)S(1)} collective-permute-done((bf16[2,24,512]{2,1,0:T(8,128)(2,1)S(1)}, bf16[2,24,512]{2,1,0:T(8,128)(2,1)S(1)}, u32[]{:S(2)}, u32[]{:S(2)}) %collective-permute-start.5) | collective-permute-done | bytes 49184 | tf_op jit(solution)/shard_map/ppermute | solution.py:94
  34.7 0.7 collective-permute-start.7
  35.4 0.1 multiply_add_fusion.3
  35.5 2.7 %collective-permute-start.11 = (f16[2,24,1536]{2,1,0:T(8,128)(2,1)S(1)}, f16[2,24,1536]{2,1,0:T(8,128)(2,1)S(1)}, u32[]{:S(2)}, u32[]{:S(2)}) collective-permute-start(f16[2,24,1536]{2,1,0:T(8,128)(2,1)S(1)} %get-tuple-element.108), channel_id=1, source_target_pairs={{0,8},{1,9},{2,10},{3,11},{4,12},{5,13},{6,14},{7,15},{8,0},{9,1},... | collective-permute-start | bytes 442376 | tf_op jit(solution)/shard_map/ppermute | solution.py:94
  38.2 2.2 %collective-permute-done.7 = bf16[2,2,24,512]{3,2,1,0:T(8,128)(2,1)S(1)} collective-permute-done((bf16[2,2,24,512]{3,2,1,0:T(8,128)(2,1)S(1)}, bf16[2,2,24,512]{3,2,1,0:T(8,128)(2,1)S(1)}, u32[]{:S(2)}, u32[]{:S(2)}) %collective-permute-start.7) | collective-permute-done | bytes 98336 | tf_op jit(solution)/shard_map/ppermute | solution.py:94
  40.4 2.3 %collective-permute-start.9 = (bf16[192,512]{1,0:T(8,128)(2,1)S(1)}, bf16[192,512]{1,0:T(8,128)(2,1)S(1)}, u32[]{:S(2)}, u32[]{:S(2)}) collective-permute-start(bf16[192,512]{1,0:T(8,128)(2,1)S(1)} %bitcast.132), channel_id=1, source_target_pairs={{0,1},{1,0},{2,3},{3,2},{4,5},{5,4},{6,7},{7,6},{8,9},{9,8},{10,11... | collective-permute-start | bytes 589832 | tf_op jit(solution)/shard_map/ppermute | solution.py:18
  42.8 2.2 %collective-permute-start.13 = (f16[2,24,1536]{2,1,0:T(8,128)(2,1)S(1)}, f16[2,24,1536]{2,1,0:T(8,128)(2,1)S(1)}, u32[]{:S(2)}, u32[]{:S(2)}) collective-permute-start(f16[2,24,1536]{2,1,0:T(8,128)(2,1)S(1)} %get-tuple-element.110), channel_id=1, source_target_pairs={{0,8},{1,9},{2,10},{3,11},{4,12},{5,13},{6,14},{7,15},{8,0},{9,1},... | collective-permute-start | bytes 442376 | tf_op jit(solution)/shard_map/ppermute | solution.py:94
  45.2 0.2 reshape.141
  45.3 0.4 fusion.72
  45.8 0.1 divide_convert_fusion.1
  45.9 0.2 fusion.45
  46.2 0.2 reshape.142
  46.4 0.9 %collective-permute-start.12 = (bf16[2,24,1536]{2,1,0:T(8,128)(2,1)S(1)}, bf16[2,24,1536]{2,1,0:T(8,128)(2,1)S(1)}, u32[]{:S(2)}, u32[]{:S(2)}) collective-permute-start(bf16[2,24,1536]{2,1,0:T(8,128)(2,1)S(1)} %reshape.142), channel_id=1, source_target_pairs={{0,8},{1,9},{2,10},{3,11},{4,12},{5,13},{6,14},{7,15},{8,0},{9,1},... | collective-permute-start | bytes 442376 | tf_op jit(solution)/shard_map/ppermute | solution.py:94
  47.3 9.6 %collective-permute-done.13 = f16[2,24,1536]{2,1,0:T(8,128)(2,1)S(1)} collective-permute-done((f16[2,24,1536]{2,1,0:T(8,128)(2,1)S(1)}, f16[2,24,1536]{2,1,0:T(8,128)(2,1)S(1)}, u32[]{:S(2)}, u32[]{:S(2)}) %collective-permute-start.13) | collective-permute-done | bytes 147488 | tf_op jit(solution)/shard_map/ppermute | solution.py:94
  56.9 0.2 reshape.143
  57.1 0.4 fusion.75
  57.6 0.1 divide_convert_fusion
  57.7 0.2 fusion.46
  58.0 0.2 reshape.144
  58.2 0.1 collective-permute-start.15
  58.2 1.5 %collective-permute-done.12 = bf16[2,24,1536]{2,1,0:T(8,128)(2,1)S(1)} collective-permute-done((bf16[2,24,1536]{2,1,0:T(8,128)(2,1)S(1)}, bf16[2,24,1536]{2,1,0:T(8,128)(2,1)S(1)}, u32[]{:S(2)}, u32[]{:S(2)}) %collective-permute-start.12) | collective-permute-done | bytes 147488 | tf_op jit(solution)/shard_map/ppermute | solution.py:94
  59.8 1.4 %collective-permute-start.14 = (bf16[2,2,24,1536]{3,2,0,1:T(8,128)(2,1)S(1)}, bf16[2,2,24,1536]{3,2,0,1:T(8,128)(2,1)S(1)}, u32[]{:S(2)}, u32[]{:S(2)}) collective-permute-start(bf16[2,2,24,1536]{3,2,0,1:T(8,128)(2,1)S(1)} %pad_maximum_fusion.5), channel_id=1, source_target_pairs={{0,4},{1,3},{2,6},{3,1},{4,0},{5,7},{6,2},{7,5},{8,12},{9,11},{10,... | collective-permute-start | bytes 884744 | tf_op jit(solution)/shard_map/ppermute | solution.py:94
  61.1 5.2 %collective-permute-done.15 = bf16[2,24,1536]{2,1,0:T(8,128)(2,1)S(1)} collective-permute-done((bf16[2,24,1536]{2,1,0:T(8,128)(2,1)S(1)}, bf16[2,24,1536]{2,1,0:T(8,128)(2,1)S(1)}, u32[]{:S(2)}, u32[]{:S(2)}) %collective-permute-start.15) | collective-permute-done | bytes 147488 | tf_op jit(solution)/shard_map/ppermute | solution.py:94
  66.4 2.7 %collective-permute-done.14 = bf16[2,2,24,1536]{3,2,0,1:T(8,128)(2,1)S(1)} collective-permute-done((bf16[2,2,24,1536]{3,2,0,1:T(8,128)(2,1)S(1)}, bf16[2,2,24,1536]{3,2,0,1:T(8,128)(2,1)S(1)}, u32[]{:S(2)}, u32[]{:S(2)}) %collective-permute-start.14) | collective-permute-done | bytes 294944 | tf_op jit(solution)/shard_map/ppermute | solution.py:94
  69.2 1.5 %collective-permute-start.16 = (bf16[2,2,2,24,1536]{4,3,0,2,1:T(8,128)(2,1)S(1)}, bf16[2,2,2,24,1536]{4,3,0,2,1:T(8,128)(2,1)S(1)}, u32[]{:S(2)}, u32[]{:S(2)}) collective-permute-start(bf16[2,2,2,24,1536]{4,3,0,2,1:T(8,128)(2,1)S(1)} %pad_maximum_fusion.3), channel_id=1, source_target_pairs={{0,2},{1,5},{2,0},{3,7},{4,6},{5,1},{6,4},{7,3},{8,10},{9,13},{10,... | collective-permute-start | bytes 1769480 | tf_op jit(solution)/shard_map/ppermute | solution.py:94
  70.7 4.9 %collective-permute-done.17 = bf16[2,2,24,1536]{3,2,0,1:T(8,128)(2,1)S(1)} collective-permute-done((bf16[2,2,24,1536]{3,2,0,1:T(8,128)(2,1)S(1)}, bf16[2,2,24,1536]{3,2,0,1:T(8,128)(2,1)S(1)}, u32[]{:S(2)}, u32[]{:S(2)}) %collective-permute-start.17) | collective-permute-done | bytes 294944 | tf_op jit(solution)/shard_map/ppermute | solution.py:94
  75.7 2.9 %collective-permute-start.18 = (bf16[2,2,2,24,1536]{4,3,0,2,1:T(8,128)(2,1)S(1)}, bf16[2,2,2,24,1536]{4,3,0,2,1:T(8,128)(2,1)S(1)}, u32[]{:S(2)}, u32[]{:S(2)}) collective-permute-start(bf16[2,2,2,24,1536]{4,3,0,2,1:T(8,128)(2,1)S(1)} %pad_maximum_fusion.4), channel_id=1, source_target_pairs={{0,2},{1,5},{2,0},{3,7},{4,6},{5,1},{6,4},{7,3},{8,10},{9,13},{10,... | collective-permute-start | bytes 1769480 | tf_op jit(solution)/shard_map/ppermute | solution.py:94
  78.6 0.6 collective-permute-done.16
  79.2 0.1 select_bitcast_fusion.3
  79.3 0.1 pad_maximum_fusion.1
  79.4 0.1 copy.24
  79.6 5.9 %fusion.2 = f32[384,2304]{1,0:T(8,128)S(1)} fusion(bf16[384,1536]{1,0:T(8,128)(2,1)S(1)} %bitcast.126, bf16[3072,2304]{1,0:T(8,128)(2,1)} %param.7), kind=kOutput, calls=%fused_computation.2 | convolution fusion | flops 2717908992 | bytes 11796480 | tf_op jit(solution)/shard_map/dot_general | solution.py:230
  85.4 1.0 %collective-permute-done.18 = bf16[2,2,2,24,1536]{4,3,0,2,1:T(8,128)(2,1)S(1)} collective-permute-done((bf16[2,2,2,24,1536]{4,3,0,2,1:T(8,128)(2,1)S(1)}, bf16[2,2,2,24,1536]{4,3,0,2,1:T(8,128)(2,1)S(1)}, u32[]{:S(2)}, u32[]{:S(2)}) %collective-permute-start.18) | collective-permute-done | bytes 589856 | tf_op jit(solution)/shard_map/ppermute | solution.py:94
  86.4 0.1 select_bitcast_fusion
  86.5 0.1 pad_maximum_fusion.2
  86.7 1.5 %fusion.22 = bf16[192,2304]{1,0:T(8,128)(2,1)S(1)} fusion(bf16[192,1536]{1,0:T(8,128)(2,1)S(1)} %bitcast.136, bf16[3072,2304]{1,0:T(8,128)(2,1)S(1)} %bitcast.138, f32[384,2304]{1,0:T(8,128)S(1)} %fusion.2), kind=kOutput, calls=%fused_computation.18 | convolution fusion | flops 1359839232 | bytes 10321920 | tf_op jit(solution)/shard_map/dot_general | solution.py:234
  88.3 1.5 %fusion.19 = f32[192,2304]{1,0:T(8,128)S(1)} fusion(bf16[192,1536]{1,0:T(8,128)(2,1)S(1)} %bitcast.135, bf16[3072,2304]{1,0:T(8,128)(2,1)S(1)} %bitcast.138, f32[384,2304]{1,0:T(8,128)S(1)} %fusion.2), kind=kOutput, calls=%fused_computation.17 | convolution fusion | flops 1359396864 | bytes 11206656 | tf_op jit(solution)/shard_map/dot_general | solution.py:238
  89.9 0.9 collective-permute-done.19
  90.7 1.1 %add_convert_fusion = bf16[192,2304]{1,0:T(8,128)(2,1)} fusion(f32[192,2304]{1,0:T(8,128)S(1)} %fusion.19, bf16[192,2304]{1,0:T(8,128)(2,1)S(1)} %collective-permute-done.19), kind=kLoop, calls=%fused_computation.24 | loop fusion | flops 1327104 | bytes 3538944 | tf_op jit(solution)/shard_map/convert_element_type | solution.py:239
  (59 shorter events, 1.5 us)
Async XLA Ops:
  0.0 6.7 %copy-start = (bf16[192,2304]{1,0:T(8,128)(2,1)S(1)}, bf16[192,2304]{1,0:T(8,128)(2,1)}, u32[]{:S(2)}) copy-start(bf16[192,2304]{1,0:T(8,128)(2,1)} %x.1) | copy-start | bytes 2654212
  0.0 6.7 %collective-permute-start.1 = (bf16[192,2304]{1,0:T(8,128)(2,1)}, bf16[192,2304]{1,0:T(8,128)(2,1)S(1)}, u32[]{:S(2)}, u32[]{:S(2)}) collective-permute-start(bf16[192,2304]{1,0:T(8,128)(2,1)} %x.1), channel_id=1, source_target_pairs={{0,1},{1,0},{2,3},{3,2},{4,5},{5,4},{6,7},{7,6},{8,9},{9,8},{10,11... | collective-permute-start | bytes 2654216 | tf_op jit(solution)/shard_map/ppermute | solution.py:18
  3.8 7.9 %collective-permute-start = (f32[96,512]{1,0:T(8,128)}, f32[96,512]{1,0:T(8,128)S(1)}, u32[]{:S(2)}, u32[]{:S(2)}) collective-permute-start(f32[96,512]{1,0:T(8,128)} %get-tuple-element.50), channel_id=1, source_target_pairs={{0,2},{1,5},{2,0},{3,7},{4,6},{5,1},{6,4},{7,3},{8,10},{9,13},{10,... | collective-permute-start | bytes 589832 | tf_op jit(solution)/shard_map/ppermute | solution.py:94
  6.9 4.7 %copy-start.1 = (f32[96,512]{1,0:T(8,128)S(1)}, f32[96,512]{1,0:T(8,128)}, u32[]{:S(2)}) copy-start(f32[96,512]{1,0:T(8,128)} %get-tuple-element.52) | copy-start | bytes 589828
  6.9 7.1 %copy-start.2 = (bf16[2304,3072]{1,0:T(8,128)(2,1)S(1)}, bf16[2304,3072]{1,0:T(8,128)(2,1)}, u32[]{:S(2)}) copy-start(bf16[2304,3072]{1,0:T(8,128)(2,1)} %param.5) | copy-start | bytes 42467332
  11.7 7.0 %collective-permute-start.2 = (f32[2,24,512]{2,1,0:T(8,128)S(1)}, f32[2,24,512]{2,1,0:T(8,128)S(1)}, u32[]{:S(2)}, u32[]{:S(2)}) collective-permute-start(f32[2,24,512]{2,1,0:T(8,128)S(1)} %get-tuple-element.117), channel_id=1, source_target_pairs={{0,4},{1,3},{2,6},{3,1},{4,0},{5,7},{6,2},{7,5},{8,12},{9,11},{10,... | collective-permute-start | bytes 294920 | tf_op jit(solution)/shard_map/ppermute | solution.py:94
  13.4 9.9 %collective-permute-start.4 = (f16[192,1536]{1,0:T(8,128)(2,1)S(1)}, f16[192,1536]{1,0:T(8,128)(2,1)S(1)}, u32[]{:S(2)}, u32[]{:S(2)}) collective-permute-start(f16[192,1536]{1,0:T(8,128)(2,1)S(1)} %fusion.34), channel_id=1, source_target_pairs={{0,2},{1,5},{2,0},{3,7},{4,6},{5,1},{6,4},{7,3},{8,10},{9,13},{10,... | collective-permute-start | bytes 1769480 | tf_op jit(solution)/shard_map/ppermute | solution.py:94
  17.3 14.2 %collective-permute-start.6 = (f16[192,1536]{1,0:T(8,128)(2,1)S(1)}, f16[192,1536]{1,0:T(8,128)(2,1)S(1)}, u32[]{:S(2)}, u32[]{:S(2)}) collective-permute-start(f16[192,1536]{1,0:T(8,128)(2,1)S(1)} %fusion.31), channel_id=1, source_target_pairs={{0,2},{1,5},{2,0},{3,7},{4,6},{5,1},{6,4},{7,3},{8,10},{9,13},{10,... | collective-permute-start | bytes 1769480 | tf_op jit(solution)/shard_map/ppermute | solution.py:94
  18.7 6.4 %collective-permute-start.3 = (f32[2,24,512]{2,1,0:T(8,128)S(1)}, f32[2,24,512]{2,1,0:T(8,128)S(1)}, u32[]{:S(2)}, u32[]{:S(2)}) collective-permute-start(f32[2,24,512]{2,1,0:T(8,128)S(1)} %add.140), channel_id=1, source_target_pairs={{0,8},{1,9},{2,10},{3,11},{4,12},{5,13},{6,14},{7,15},{8,0},{9,1},... | collective-permute-start | bytes 294920 | tf_op jit(solution)/shard_map/ppermute | solution.py:94
  23.6 11.8 %collective-permute-start.8 = (f16[2,2,24,1536]{3,2,0,1:T(8,128)(2,1)S(1)}, f16[2,2,24,1536]{3,2,0,1:T(8,128)(2,1)S(1)}, u32[]{:S(2)}, u32[]{:S(2)}) collective-permute-start(f16[2,2,24,1536]{3,2,0,1:T(8,128)(2,1)S(1)} %fusion.50), channel_id=1, source_target_pairs={{0,4},{1,3},{2,6},{3,1},{4,0},{5,7},{6,2},{7,5},{8,12},{9,11},{10,... | collective-permute-start | bytes 884744 | tf_op jit(solution)/shard_map/ppermute | solution.py:94
  25.2 9.5 %collective-permute-start.5 = (bf16[2,24,512]{2,1,0:T(8,128)(2,1)S(1)}, bf16[2,24,512]{2,1,0:T(8,128)(2,1)S(1)}, u32[]{:S(2)}, u32[]{:S(2)}) collective-permute-start(bf16[2,24,512]{2,1,0:T(8,128)(2,1)S(1)} %add_convert_fusion.3), channel_id=1, source_target_pairs={{0,4},{1,3},{2,6},{3,1},{4,0},{5,7},{6,2},{7,5},{8,12},{9,11},{10,... | collective-permute-start | bytes 147464 | tf_op jit(solution)/shard_map/ppermute | solution.py:94
  31.9 10.8 %collective-permute-start.10 = (f16[2,2,24,1536]{3,2,0,1:T(8,128)(2,1)S(1)}, f16[2,2,24,1536]{3,2,0,1:T(8,128)(2,1)S(1)}, u32[]{:S(2)}, u32[]{:S(2)}) collective-permute-start(f16[2,2,24,1536]{3,2,0,1:T(8,128)(2,1)S(1)} %fusion.51), channel_id=1, source_target_pairs={{0,4},{1,3},{2,6},{3,1},{4,0},{5,7},{6,2},{7,5},{8,12},{9,11},{10,... | collective-permute-start | bytes 884744 | tf_op jit(solution)/shard_map/ppermute | solution.py:94
  34.7 5.7 %collective-permute-start.7 = (bf16[2,2,24,512]{3,2,1,0:T(8,128)(2,1)S(1)}, bf16[2,2,24,512]{3,2,1,0:T(8,128)(2,1)S(1)}, u32[]{:S(2)}, u32[]{:S(2)}) collective-permute-start(bf16[2,2,24,512]{3,2,1,0:T(8,128)(2,1)S(1)} %pad_maximum_fusion.8), channel_id=1, source_target_pairs={{0,2},{1,5},{2,0},{3,7},{4,6},{5,1},{6,4},{7,3},{8,10},{9,13},{10,... | collective-permute-start | bytes 294920 | tf_op jit(solution)/shard_map/ppermute | solution.py:94
  35.5 9.6 %collective-permute-start.11 = (f16[2,24,1536]{2,1,0:T(8,128)(2,1)S(1)}, f16[2,24,1536]{2,1,0:T(8,128)(2,1)S(1)}, u32[]{:S(2)}, u32[]{:S(2)}) collective-permute-start(f16[2,24,1536]{2,1,0:T(8,128)(2,1)S(1)} %get-tuple-element.108), channel_id=1, source_target_pairs={{0,8},{1,9},{2,10},{3,11},{4,12},{5,13},{6,14},{7,15},{8,0},{9,1},... | collective-permute-start | bytes 442376 | tf_op jit(solution)/shard_map/ppermute | solution.py:94
  40.4 4.6 %collective-permute-start.9 = (bf16[192,512]{1,0:T(8,128)(2,1)S(1)}, bf16[192,512]{1,0:T(8,128)(2,1)S(1)}, u32[]{:S(2)}, u32[]{:S(2)}) collective-permute-start(bf16[192,512]{1,0:T(8,128)(2,1)S(1)} %bitcast.132), channel_id=1, source_target_pairs={{0,1},{1,0},{2,3},{3,2},{4,5},{5,4},{6,7},{7,6},{8,9},{9,8},{10,11... | collective-permute-start | bytes 589832 | tf_op jit(solution)/shard_map/ppermute | solution.py:18
  42.8 14.1 %collective-permute-start.13 = (f16[2,24,1536]{2,1,0:T(8,128)(2,1)S(1)}, f16[2,24,1536]{2,1,0:T(8,128)(2,1)S(1)}, u32[]{:S(2)}, u32[]{:S(2)}) collective-permute-start(f16[2,24,1536]{2,1,0:T(8,128)(2,1)S(1)} %get-tuple-element.110), channel_id=1, source_target_pairs={{0,8},{1,9},{2,10},{3,11},{4,12},{5,13},{6,14},{7,15},{8,0},{9,1},... | collective-permute-start | bytes 442376 | tf_op jit(solution)/shard_map/ppermute | solution.py:94
  46.4 13.3 %collective-permute-start.12 = (bf16[2,24,1536]{2,1,0:T(8,128)(2,1)S(1)}, bf16[2,24,1536]{2,1,0:T(8,128)(2,1)S(1)}, u32[]{:S(2)}, u32[]{:S(2)}) collective-permute-start(bf16[2,24,1536]{2,1,0:T(8,128)(2,1)S(1)} %reshape.142), channel_id=1, source_target_pairs={{0,8},{1,9},{2,10},{3,11},{4,12},{5,13},{6,14},{7,15},{8,0},{9,1},... | collective-permute-start | bytes 442376 | tf_op jit(solution)/shard_map/ppermute | solution.py:94
  58.2 8.1 %collective-permute-start.15 = (bf16[2,24,1536]{2,1,0:T(8,128)(2,1)S(1)}, bf16[2,24,1536]{2,1,0:T(8,128)(2,1)S(1)}, u32[]{:S(2)}, u32[]{:S(2)}) collective-permute-start(bf16[2,24,1536]{2,1,0:T(8,128)(2,1)S(1)} %reshape.144), channel_id=1, source_target_pairs={{0,8},{1,9},{2,10},{3,11},{4,12},{5,13},{6,14},{7,15},{8,0},{9,1},... | collective-permute-start | bytes 442376 | tf_op jit(solution)/shard_map/ppermute | solution.py:94
  59.8 9.3 %collective-permute-start.14 = (bf16[2,2,24,1536]{3,2,0,1:T(8,128)(2,1)S(1)}, bf16[2,2,24,1536]{3,2,0,1:T(8,128)(2,1)S(1)}, u32[]{:S(2)}, u32[]{:S(2)}) collective-permute-start(bf16[2,2,24,1536]{3,2,0,1:T(8,128)(2,1)S(1)} %pad_maximum_fusion.5), channel_id=1, source_target_pairs={{0,4},{1,3},{2,6},{3,1},{4,0},{5,7},{6,2},{7,5},{8,12},{9,11},{10,... | collective-permute-start | bytes 884744 | tf_op jit(solution)/shard_map/ppermute | solution.py:94
  66.4 9.2 %collective-permute-start.17 = (bf16[2,2,24,1536]{3,2,0,1:T(8,128)(2,1)S(1)}, bf16[2,2,24,1536]{3,2,0,1:T(8,128)(2,1)S(1)}, u32[]{:S(2)}, u32[]{:S(2)}) collective-permute-start(bf16[2,2,24,1536]{3,2,0,1:T(8,128)(2,1)S(1)} %pad_maximum_fusion.6), channel_id=1, source_target_pairs={{0,4},{1,3},{2,6},{3,1},{4,0},{5,7},{6,2},{7,5},{8,12},{9,11},{10,... | collective-permute-start | bytes 884744 | tf_op jit(solution)/shard_map/ppermute | solution.py:94
  69.2 9.9 %collective-permute-start.16 = (bf16[2,2,2,24,1536]{4,3,0,2,1:T(8,128)(2,1)S(1)}, bf16[2,2,2,24,1536]{4,3,0,2,1:T(8,128)(2,1)S(1)}, u32[]{:S(2)}, u32[]{:S(2)}) collective-permute-start(bf16[2,2,2,24,1536]{4,3,0,2,1:T(8,128)(2,1)S(1)} %pad_maximum_fusion.3), channel_id=1, source_target_pairs={{0,2},{1,5},{2,0},{3,7},{4,6},{5,1},{6,4},{7,3},{8,10},{9,13},{10,... | collective-permute-start | bytes 1769480 | tf_op jit(solution)/shard_map/ppermute | solution.py:94
  75.7 10.8 %collective-permute-start.18 = (bf16[2,2,2,24,1536]{4,3,0,2,1:T(8,128)(2,1)S(1)}, bf16[2,2,2,24,1536]{4,3,0,2,1:T(8,128)(2,1)S(1)}, u32[]{:S(2)}, u32[]{:S(2)}) collective-permute-start(bf16[2,2,2,24,1536]{4,3,0,2,1:T(8,128)(2,1)S(1)} %pad_maximum_fusion.4), channel_id=1, source_target_pairs={{0,2},{1,5},{2,0},{3,7},{4,6},{5,1},{6,4},{7,3},{8,10},{9,13},{10,... | collective-permute-start | bytes 1769480 | tf_op jit(solution)/shard_map/ppermute | solution.py:94
  79.4 7.3 %slice-start = ((s8[14155776]{0:T(1024)(128)(4,1)}), s8[4194304]{0:T(1024)(128)(4,1)S(1)}, s32[]{:S(2)}) async-start(s8[14155776]{0:T(1024)(128)(4,1)} %bitcast.137), calls=%async_computation | async-start | bytes 8388608
  79.5 7.1 %slice-start.1 = ((s8[14155776]{0:T(1024)(128)(4,1)}), s8[4194304]{0:T(1024)(128)(4,1)S(1)}, s32[]{:S(2)}) async-start(s8[14155776]{0:T(1024)(128)(4,1)} %bitcast.137), calls=%async_computation.1 | async-start | bytes 8388608
  79.5 7.1 %slice-start.2 = ((s8[14155776]{0:T(1024)(128)(4,1)}), s8[4194304]{0:T(1024)(128)(4,1)S(1)}, s32[]{:S(2)}) async-start(s8[14155776]{0:T(1024)(128)(4,1)} %bitcast.137), calls=%async_computation.2 | async-start | bytes 8388608
  79.5 7.1 %slice-start.3 = ((s8[14155776]{0:T(1024)(128)(4,1)}), s8[1572864]{0:T(1024)(128)(4,1)S(1)}, s32[]{:S(2)}) async-start(s8[14155776]{0:T(1024)(128)(4,1)} %bitcast.137), calls=%async_computation.3 | async-start | bytes 3145728
  88.2 2.5 %collective-permute-start.19 = (bf16[192,2304]{1,0:T(8,128)(2,1)S(1)}, bf16[192,2304]{1,0:T(8,128)(2,1)S(1)}, u32[]{:S(2)}, u32[]{:S(2)}) collective-permute-start(bf16[192,2304]{1,0:T(8,128)(2,1)S(1)} %fusion.22), channel_id=1, source_target_pairs={{0,1},{1,0},{2,3},{3,2},{4,5},{5,4},{6,7},{7,6},{8,9},{9,8},{10,11... | collective-permute-start | bytes 2654216 | tf_op jit(solution)/shard_map/ppermute | solution.py:18
